TPU v7x, 32 devices: a whole 2x2x4 slice. The times are simulated.
32 devices in a mesh: row: 4 (over y, x), seq: 8 (over z, core).
Axes of the slice: x: 2, y: 2, z: 4, core: 2. Of those that a mesh axis runs over, the one named last changes fastest.
Arguments:
- tokens: bfloat16 [16, 2048, 2048], P('row', 'seq'), may hold values from -6 to 6
- lengths: int32 [16], P('row'), may hold values from 64 to 2048, as said below
- cotangent: bfloat16 [16, 2048, 2048], P('row', 'seq'), may hold values from -6 to 6
- w_qkv: bfloat16 [2048, 1536], P(('row', 'seq')), may hold values from -0.125 to 0.125
- w_out: bfloat16 [2048, 1024], P(('row', 'seq')), may hold values from -1.5 to 1.5
- w_gateup: bfloat16 [2048, 2048], P(('row', 'seq')), may hold values from -0.125 to 0.125
- w_down: bfloat16 [2048, 1024], P(('row', 'seq')), may hold values from -0.1875 to 0.1875
- norm_attn: bfloat16 [2048], P(('row', 'seq')), may hold values from 0.5 to 1.5
- norm_ffn: bfloat16 [2048], P(('row', 'seq')), may hold values from 0.5 to 1.5
- q_gain: bfloat16 [64], replicated, may hold values from 0.099609375 to 1.8984375
- k_gain: bfloat16 [64], replicated, may hold values from 0.099609375 to 1.8984375
Outputs:
- output: bfloat16 [16, 2048, 2048], P('row', 'seq')
- grad_tokens: bfloat16 [16, 2048, 2048], P('row', 'seq')
- grad_qkv: float32 [2048, 1536], P(('row', 'seq'))
- grad_out: float32 [2048, 1024], P(('row', 'seq'))
- grad_gateup: float32 [2048, 2048], P(('row', 'seq'))
- grad_down: float32 [2048, 1024], P(('row', 'seq'))
- grad_norm_attn: float32 [2048], P(('row', 'seq'))
- grad_norm_ffn: float32 [2048], P(('row', 'seq'))
- grad_q_gain: float32 [64], replicated
- grad_k_gain: float32 [64], replicated
Inputs may be any that keep to these rules, and one draw needn't show every extreme that they name: `lengths`: each aligned block of 4 entries (the sequences of one index of row) holds at least one entry equal to 2048; the others are heavy-tailed.
All inputs are finite; a program needn't handle non-finite values.
Results may differ from a plain program's by a relative error of at most 0.033.
Values may be sent and summed in bfloat16 or wider, within the bound.
No kernel may reach another device: no remote copies, remote signals or barrier semaphores. Data moves between devices by JAX's collectives and lax.ppermute only.
A program may use at most 448 MiB of HBM per device.

v0:
```python
import functools
import math

import jax
import jax.numpy as jnp
from jax import lax
from jax.experimental import pallas as pl
from jax.experimental.pallas import tpu as pltpu
from jax.sharding import PartitionSpec as P

norm_eps = 1e-06
theta_base = 10000.0
both = ("row", "seq")
f32 = jnp.float32
bf16 = jnp.bfloat16
vmem_cap = 56 * 1024 * 1024
any_spec = pl.BlockSpec(memory_space=pl.ANY)
NN = (((1,), (0,)), ((), ()))
NT = (((1,), (1,)), ((), ()))
TN = (((0,), (0,)), ((), ()))


def mm(left, right, dims=NN):
    return lax.dot_general(left, right, dims, preferred_element_type=f32)


def after(value, *earlier):
    return lax.optimization_barrier((value, *earlier))[0]


def params(n_grid):
    return pltpu.CompilerParams(
        dimension_semantics=("arbitrary",) * n_grid, vmem_limit_bytes=vmem_cap
    )


def lane_iota(shape):
    return lax.broadcasted_iota(jnp.int32, shape, len(shape) - 1)


def group_matrix(head_dim, value):
    i = lax.broadcasted_iota(jnp.int32, (128, 128), 0) // head_dim
    j = lax.broadcasted_iota(jnp.int32, (128, 128), 1) // head_dim
    return jnp.where(i == j, value, 0.0).astype(bf16)


def group_sum(values, matrix):
    high = values.astype(bf16)
    low = (values - high.astype(f32)).astype(bf16)
    return mm(high, matrix) + mm(low, matrix)


def turn(values, cos_ref, sa_ref, sb_ref):
    return (
        values * cos_ref[...]
        + pltpu.roll(values, 96, 1) * sa_ref[...]
        + pltpu.roll(values, 32, 1) * sb_ref[...]
    )


def turn_back(values, cos_ref, sa_ref, sb_ref):
    return (
        values * cos_ref[...]
        - pltpu.roll(values, 96, 1) * sa_ref[...]
        - pltpu.roll(values, 32, 1) * sb_ref[...]
    )


class Grid:
    def __init__(self, rows, seqs):
        self.rows, self.seqs, self.depth = rows, seqs, seqs // 2
        self.row = lax.axis_index("row")
        seq = lax.axis_index("seq")
        self.level, self.core = seq // 2, lax.rem(seq, 2)
        self.seq = seq
        bits = [1 << k for k in range(rows.bit_length() - 1)]
        self.orders = (bits, bits[::-1])
        self.place = jnp.stack([self.row, self.level, self.core]).astype(jnp.int32)

    def move(self, value, where):
        pairs = []
        for row in range(self.rows):
            for seq in range(self.seqs):
                target = where(row, seq)
                if target is not None:
                    pairs.append((row * self.seqs + seq, target[0] * self.seqs + target[1]))
        return lax.ppermute(value, both, pairs)

    def across(self, value, mask):
        return self.move(value, lambda r, s: (r ^ mask, s))

    def partner(self, value):
        return self.move(value, lambda r, s: (r, s ^ 1))

    def around(self, value):
        return self.move(value, lambda r, s: (r, (s + 2) % self.seqs))

    def up(self, value):
        return self.move(value, lambda r, s: (r, s + 2) if s + 2 < self.seqs else None)

    def down(self, value):
        return self.move(value, lambda r, s: (r, s - 2) if s >= 2 else None)

    def masks(self, half):
        found = [0]
        for bit in self.orders[half]:
            found = found + [m ^ bit for m in found]
        return found

    def ring(self, shard, waits=()):
        steps = [shard]
        for hop in range(self.depth - 1):
            held = steps[-1]
            if hop < len(waits):
                held = after(held, *waits[hop])
            steps.append(self.around(held))
        return steps

    def spread(self, steps, waits=()):
        middle = self.depth // 2
        held = [jnp.stack(steps[:middle])[None], jnp.stack(steps[middle:])[None]]
        pieces = []
        arrived = []
        for stage in range(len(self.orders[0])):
            for half in range(2):
                if stage < len(waits):
                    held[half] = after(held[half], *waits[stage])
            found = [self.across(held[half], self.orders[half][stage]) for half in range(2)]
            arrived.append(found)
            if stage == len(self.orders[0]) - 1:
                pieces = [held[0], found[0], held[1], found[1]]
            else:
                held = [jnp.concatenate([held[k], found[k]], axis=0) for k in range(2)]
        return pieces, arrived

    def with_partner(self, pieces, merge):
        if merge:
            pieces = [jnp.stack(pieces)]
        return pieces + [self.partner(p) for p in pieces]

    def everywhere(self, value):
        for bit in self.orders[0]:
            value = value + self.across(value, bit)
        bit = 1
        while bit < self.seqs:
            value = value + self.move(value, lambda r, s, bit=bit: (r, s ^ bit))
            bit *= 2
        return value


class Order:
    def __init__(self):
        self.kernel = None
        self.waits = []

    def pin(self, *values):
        self.waits += values

    def enter(self, value):
        return after(value, *self.waits) if self.waits else value

    def leave(self, value):
        self.kernel = value
        self.waits = [value]

    def late(self, value):
        return after(value, self.kernel)


class Sum:
    def __init__(self, grid, order, parts):
        mine, self.theirs = parts
        self.grid = grid
        self.order = order
        self.halves = [[mine[half]] for half in range(2)]
        self.stage = 0
        self.flight = []
        self.row_stages = len(grid.orders[0])
        self.total = None

    def at(self, step):
        depth = self.grid.depth
        index = lax.rem(self.grid.level - step + 2 * depth, depth)
        return lax.dynamic_index_in_dim(self.levels, index, 0, keepdims=False)

    def land(self):
        came, self.flight = [self.order.late(c) for c in self.flight], []
        if came:
            if self.stage == 1:
                for half in range(2):
                    self.halves[half].append(came[0][half])
            elif self.stage <= 1 + self.row_stages:
                for half in range(2):
                    self.halves[half].append(came[half])
            else:
                self.total = came[0].astype(f32) + self.at(self.stage - self.row_stages)
        return came

    def go(self):
        grid, late = self.grid, self.order.late
        self.land()
        if self.stage == 0:
            sent = [self.theirs]
            self.flight = [grid.partner(self.theirs)]
        elif self.stage <= self.row_stages:
            sent = []
            for half in range(2):
                parts = self.halves[half]
                bit = grid.orders[half][::-1][self.stage - 1]
                count = parts[0].shape[0] // 2
                if half == 0:
                    kept, given = slice(0, count), slice(count, None)
                else:
                    kept, given = slice(0, None, 2), slice(1, None, 2)
                value = sum(p[given].astype(f32) for p in parts).astype(bf16)
                self.halves[half] = [p[kept] for p in parts]
                sent.append(late(value))
                self.flight.append(grid.across(sent[half], bit))
        elif self.stage < self.row_stages + grid.depth:
            if self.total is None:
                self.levels = jnp.concatenate(
                    [sum(p[0].astype(f32) for p in parts) for parts in self.halves], axis=0
                )
                self.total = self.at(1)
            sent = [late(self.total.astype(bf16))]
            self.flight = [grid.around(sent[0])]
        else:
            return []
        self.stage += 1
        return sent

    def finish(self):
        while self.go():
            pass
        return self.total


def loads(grid, place_ref, pieces, target, sems, columns=None, at_column=0):
    row, level, core = place_ref[0], place_ref[1], place_ref[2]
    shard, columns_all = pieces[0].shape[-2:]
    if columns is None:
        columns = (0, columns_all)
    width = columns[1] - columns[0]
    merged = len(pieces) == 2
    copies = []
    for which in range(8):
        ref = pieces[which // 4].at[which % 4] if merged else pieces[which]
        half = which // 2 % 2
        whose = core if which < 4 else 1 - core
        first = 0 if half == 0 else grid.depth // 2
        masks = grid.masks(half)
        masks = masks[len(masks) // 2 :] if which % 2 else masks[: len(masks) // 2]
        for m, mask in enumerate(masks):
            for h in range(ref.shape[1]):
                at_level = lax.rem(level - (first + h) + grid.depth, grid.depth)
                start = ((row ^ mask) * grid.seqs + at_level * 2 + whose) * shard
                copies.append(
                    pltpu.make_async_copy(
                        ref.at[m, h, :, columns[0] : columns[1]],
                        target.at[
                            pl.ds(pl.multiple_of(start, shard), shard),
                            at_column : at_column + width,
                        ],
                        sems.at[len(copies)],
                    )
                )
    return copies


def n_loads(grid):
    return grid.rows * grid.seqs


def project_kernel(grid, normed_slabs, head_dim, with_scale, place_ref, tok_ref, *rest):
    pieces, rest = rest[:2], rest[2:]
    gain_ref, cos_ref, sa_ref, sb_ref, *rest = rest
    if with_scale:
        heads_ref, raw_ref, scale_ref, weight, sems = rest
    else:
        scale_in_ref, heads_ref, raw_ref, weight, sems = rest

    @pl.when(pl.program_id(0) == 0)
    def _():
        copies = loads(grid, place_ref, pieces, weight, sems)
        for copy in copies:
            copy.start()
        for copy in copies:
            copy.wait()

    if with_scale:
        x = tok_ref[...].astype(f32)
        scale = lax.rsqrt(jnp.mean(x * x, axis=-1, keepdims=True) + norm_eps)
        scale_ref[...] = jnp.broadcast_to(scale, scale_ref.shape)
    else:
        scale = scale_in_ref[:, :1]
    projected = mm(tok_ref[...], weight[...]) * scale
    mean_matrix = group_matrix(head_dim, 1.0 / head_dim)
    raw_ref[...] = projected[:, : raw_ref.shape[1]].astype(bf16)
    for slab in range(heads_ref.shape[1] // 128):
        lanes = slice(128 * slab, 128 * slab + 128)
        part = projected[:, lanes]
        if slab < normed_slabs:
            inverse = lax.rsqrt(group_sum(part * part, mean_matrix) + norm_eps)
            part = turn(part * inverse * gain_ref[...], cos_ref, sa_ref, sb_ref)
        heads_ref[:, lanes] = part.astype(bf16)


def project(grid, tokens, pieces, gain, tables, normed, head_dim, scale=None):
    rows, width = tokens.shape
    out_width = pieces[0].shape[-1]
    span = tables[0].shape[0]
    row_block = lambda n: pl.BlockSpec((span, n), lambda i, *_: (i, 0))
    fixed = lambda a: pl.BlockSpec(a.shape, lambda i, *_: (0,) * a.ndim)
    args = [tokens, *pieces, gain, *tables]
    in_specs = [row_block(width)] + [any_spec] * 2 + [fixed(a) for a in (gain, *tables)]
    out_shape = [
        jax.ShapeDtypeStruct((rows, out_width), bf16),
        jax.ShapeDtypeStruct((rows, normed), bf16),
    ]
    out_specs = [row_block(out_width), row_block(normed)]
    if scale is None:
        out_shape.append(jax.ShapeDtypeStruct((rows, 128), f32))
        out_specs.append(row_block(128))
    else:
        args.append(scale)
        in_specs.append(row_block(128))
    return pl.pallas_call(
        functools.partial(project_kernel, grid, normed // 128, head_dim, scale is None),
        grid_spec=pltpu.PrefetchScalarGridSpec(
            num_scalar_prefetch=1,
            grid=(rows // span,),
            in_specs=in_specs,
            out_specs=out_specs,
            scratch_shapes=[
                pltpu.VMEM((width, out_width), bf16),
                pltpu.SemaphoreType.DMA((n_loads(grid),)),
            ],
        ),
        out_shape=out_shape,
        compiler_params=params(1),
        cost_estimate=pl.CostEstimate(
            flops=4 * rows * width * out_width,
            bytes_accessed=2 * (rows * (width + 2 * out_width) + width * out_width),
            transcendentals=rows * normed,
        ),
    )(grid.place, *args)


def placed_pair(slab, parity, low):
    values = slab.astype(f32)
    rolled = pltpu.roll(values, 64, 1)
    here, there = (rolled, values) if parity else (values, rolled)
    return jnp.where(low, here, 0.0), jnp.where(low, 0.0, there)


def block_state(info_ref, seq, base, block, span):
    offset = info_ref[0]
    length = info_ref[1 + seq]
    some = (base >= 0) & (base < jnp.minimum(offset + span, length))
    whole = some & (base + block <= jnp.minimum(offset + 1, length))
    return whole, some & jnp.logical_not(whole)


def allowed(info_ref, seq, base, shape, key_axis, block, span):
    q_pos = info_ref[0] + lax.rem(
        lax.broadcasted_iota(jnp.int32, shape, 1 - key_axis), span
    )
    k_pos = base + lax.rem(lax.broadcasted_iota(jnp.int32, shape, key_axis), block)
    return (k_pos <= q_pos) & (k_pos < info_ref[1 + seq])


def chunk_copies(chunks, buffer, sems, info_ref, seq, n_seqs, slot, span, then, backward=False):
    for i, chunk in enumerate(chunks):
        base = info_ref[1 + n_seqs + i]
        needed = (base >= 0) & (base < jnp.minimum(info_ref[0] + span, info_ref[1 + seq]))
        if backward:
            needed = needed & (info_ref[0] < info_ref[1 + seq])

        @pl.when(needed)
        def _(i=i, chunk=chunk):
            then(pltpu.make_async_copy(chunk.at[seq], buffer.at[slot, i], sems.at[slot, i]))


def fetch_chunks(chunks, buffer, sems, info_ref, span, backward=False):
    seq, n_seqs = pl.program_id(0), pl.num_programs(0)
    slot = lax.rem(seq, 2)
    common = (chunks, buffer, sems, info_ref)

    @pl.when(seq == 0)
    def _():
        chunk_copies(*common, seq, n_seqs, slot, span, lambda c: c.start(), backward)

    @pl.when(seq + 1 < n_seqs)
    def _():
        chunk_copies(*common, seq + 1, n_seqs, 1 - slot, span, lambda c: c.start(), backward)

    chunk_copies(*common, seq, n_seqs, slot, span, lambda c: c.wait(), backward)
    return slot


def stacked_at(ref, head):
    first = head * 256
    return jnp.concatenate(
        [ref[0, :, first : first + 128], ref[0, :, first + 128 : first + 256]], axis=0
    )


def unstack_to(ref, head, value):
    first = head * 256
    span = ref.shape[1]
    ref[0, :, first : first + 128] = value[:span].astype(ref.dtype)
    ref[0, :, first + 128 : first + 256] = value[span:].astype(ref.dtype)


def split_lanes(values):
    lane = lax.rem(lane_iota(values.shape), 64)
    high = values.astype(bf16).astype(f32)
    rest = values - high
    return jnp.where(lane == 0, high, jnp.where(lane == 1, rest, 0.0)).astype(bf16)


def attend_kernel(n, with_acc, finish, info_ref, q_ref, *refs):
    chunks, refs = refs[:n], refs[n:]
    if with_acc:
        acc_in, refs = refs[0], refs[1:]
    if finish:
        out_ref, log_ref, buffer, sems, acc = refs
    else:
        acc_out, buffer, sems, acc = refs
    seq, n_seqs = pl.program_id(0), pl.num_programs(0)
    span = q_ref.shape[1]
    n_heads = q_ref.shape[2] // 256
    slot = fetch_chunks(chunks, buffer, sems, info_ref, span)

    def one_head(head):
        parity = head % 2
        k_lanes = slice(head // 2 * 128, head // 2 * 128 + 128)
        v_lanes = slice((n_heads + head) // 2 * 128, (n_heads + head) // 2 * 128 + 128)
        acc[...] = acc_in[0, head] if with_acc else jnp.zeros(acc.shape, f32)

        @pl.loop(0, n)
        def _(chunk):
            base = info_ref[1 + n_seqs + chunk]
            whole, partly = block_state(info_ref, seq, base, span, span)

            def step(masked):
                low = lane_iota((span, 128)) < 64
                ones_low = jnp.where(low, 1.0, 0.0).astype(bf16)
                ones_high = jnp.where(low, 0.0, 1.0).astype(bf16)
                k0, k1 = placed_pair(buffer[slot, chunk, :, k_lanes], parity, low)
                v0, v1 = placed_pair(buffer[slot, chunk, :, v_lanes], parity, low)
                k_pair = jnp.concatenate([k0, k1], axis=0).astype(bf16)
                v_pair = jnp.concatenate(
                    [
                        jnp.concatenate([v0.astype(bf16), ones_low], axis=1),
                        jnp.concatenate([v1.astype(bf16), ones_high], axis=1),
                    ],
                    axis=0,
                )
                weights = jnp.exp2(mm(stacked_at(q_ref, head), k_pair, NT))
                if masked:
                    ok = allowed(info_ref, seq, base, weights.shape, 1, span, span)
                    weights = jnp.where(ok, weights, 0.0)
                acc[...] += mm(weights.astype(bf16), v_pair)

            @pl.when(whole)
            def _():
                step(False)

            @pl.when(partly)
            def _():
                step(True)

        if finish:
            totals = acc[:, 128:]
            unstack_to(out_ref, head, acc[:, :128] / totals)
            unstack_to(log_ref, head, split_lanes(-jnp.log2(totals)))
        else:
            acc_out[0, head] = acc[...]

    for head in range(n_heads):
        one_head(head)


def attend(info, bases, queries, chunks, acc=None, finish=True):
    seqs, span, width = queries.shape
    n_heads = width // 256
    n = len(chunks)
    q_spec = pl.BlockSpec((1, span, width), lambda b, *_: (b, 0, 0))
    acc_spec = pl.BlockSpec((1, n_heads, 2 * span, 256), lambda b, *_: (b, 0, 0, 0))
    acc_shape = jax.ShapeDtypeStruct((seqs, n_heads, 2 * span, 256), f32)
    args = [queries, *chunks]
    in_specs = [q_spec] + [any_spec] * n
    if acc is not None:
        args.append(acc)
        in_specs.append(acc_spec)
    if finish:
        out_shape = [jax.ShapeDtypeStruct(queries.shape, bf16)] * 2
        out_specs = [q_spec, q_spec]
    else:
        out_shape, out_specs = acc_shape, acc_spec
    return pl.pallas_call(
        functools.partial(attend_kernel, n, acc is not None, finish),
        grid_spec=pltpu.PrefetchScalarGridSpec(
            num_scalar_prefetch=1,
            grid=(seqs,),
            in_specs=in_specs,
            out_specs=out_specs,
            scratch_shapes=[
                pltpu.VMEM((2, n, span, chunks[0].shape[2]), bf16),
                pltpu.SemaphoreType.DMA((2, n)),
                pltpu.VMEM((2 * span, 256), f32),
            ],
        ),
        out_shape=out_shape,
        compiler_params=params(1),
        cost_estimate=pl.CostEstimate(
            flops=4 * 4 * seqs * span * width * span * n,
            bytes_accessed=4 * seqs * (span * width * 3 + n * span * width // 2),
            transcendentals=seqs * span * width // 64 * span * n,
        ),
    )(jnp.concatenate([info, bases]), *args)


def attend_back_kernel(n, with_acc, finish, info_ref, q_ref, do_ref, o_ref, log_ref, *refs):
    chunks, refs = refs[:n], refs[n:]
    if with_acc:
        acc_in, refs = refs[0], refs[1:]
    grads_out, dq_ref, buffer, sems, acc, q_wide, do_wide = refs
    seq, n_seqs = pl.program_id(0), pl.num_programs(0)
    span = q_ref.shape[1]
    n_heads = q_ref.shape[2] // 256
    alive = info_ref[0] < info_ref[1 + seq]
    slot = fetch_chunks(chunks, buffer, sems, info_ref, span, True)
    grads_out[...] = jnp.zeros(grads_out.shape, grads_out.dtype)

    def one_head(head):
        parity = head % 2
        k_lanes = slice(head // 2 * 128, head // 2 * 128 + 128)
        v_lanes = slice((n_heads + head) // 2 * 128, (n_heads + head) // 2 * 128 + 128)
        acc[...] = acc_in[0, head] if with_acc else jnp.zeros(acc.shape, f32)

        @pl.when(alive)
        def _():
            heads = stacked_at(do_ref, head)
            dots = group_sum(
                heads.astype(f32) * stacked_at(o_ref, head).astype(f32), group_matrix(64, 1.0)
            )
            do_wide[:, :128] = heads
            do_wide[:, 128:] = split_lanes(-dots)
            q_wide[:, :128] = stacked_at(q_ref, head)
            q_wide[:, 128:] = stacked_at(log_ref, head)

            @pl.loop(0, n)
            def _(chunk):
                base = info_ref[1 + n_seqs + chunk]
                whole, partly = block_state(info_ref, seq, base, span, span)

                def step(masked):
                    low = lane_iota((span, 128)) < 64
                    half_lane = lax.rem(lane_iota((span, 128)), 64)
                    pick_low = jnp.where(low & (half_lane < 2), 1.0, 0.0)
                    pick_high = jnp.where(low | (half_lane >= 2), 0.0, 1.0)
                    picks = jnp.concatenate([pick_low, pick_high], axis=0).astype(bf16)
                    k0, k1 = placed_pair(buffer[slot, chunk, :, k_lanes], parity, low)
                    v0, v1 = placed_pair(buffer[slot, chunk, :, v_lanes], parity, low)
                    k_pair = jnp.concatenate([k0, k1], axis=0)
                    k_turned = jnp.transpose(k_pair).astype(bf16)
                    k_wide = jnp.concatenate([k_pair.astype(bf16), picks], axis=1)
                    v_wide = jnp.concatenate(
                        [jnp.concatenate([v0, v1], axis=0).astype(bf16), picks], axis=1
                    )
                    weights = jnp.exp2(mm(k_wide, q_wide[...], NT))
                    if masked:
                        ok = allowed(info_ref, seq, base, weights.shape, 0, span, span)
                        weights = jnp.where(ok, weights, 0.0)
                    grads = (weights * mm(v_wide, do_wide[...], NT)).astype(bf16)
                    both_v = mm(weights.astype(bf16), do_wide[:, :128])
                    both_k = mm(grads, q_wide[:, :128]) * math.log(2.0)
                    acc[...] += mm(k_turned, grads)

                    def joined(pair):
                        total = jnp.where(low, pair[:span] + pltpu.roll(pair[span:], 64, 1), 0.0)
                        return pltpu.roll(total, 64, 1) if parity else total

                    dtype = grads_out.dtype
                    grads_out[chunk, 0, :, k_lanes] += joined(both_k).astype(dtype)
                    grads_out[chunk, 0, :, v_lanes] += joined(both_v).astype(dtype)

                @pl.when(whole)
                def _():
                    step(False)

                @pl.when(partly)
                def _():
                    step(True)

        if finish:
            unstack_to(dq_ref, head, jnp.transpose(acc[...]) * 0.125)
        else:
            dq_ref[0, head] = acc[...]

    for head in range(n_heads):
        one_head(head)


def attend_back(info, bases, queries, grad_out, out, logs, chunks, acc=None, finish=True):
    seqs, span, width = queries.shape
    n_heads = width // 256
    n = len(chunks)
    q_spec = pl.BlockSpec((1, span, width), lambda b, *_: (b, 0, 0))
    acc_spec = pl.BlockSpec((1, n_heads, 128, 2 * span), lambda b, *_: (b, 0, 0, 0))
    acc_shape = jax.ShapeDtypeStruct((seqs, n_heads, 128, 2 * span), f32)
    args = [queries, grad_out, out, logs, *chunks]
    in_specs = [q_spec] * 4 + [any_spec] * n
    if acc is not None:
        args.append(acc)
        in_specs.append(acc_spec)
    kv_width = chunks[0].shape[2]
    if finish:
        dq_shape, dq_spec = jax.ShapeDtypeStruct(queries.shape, bf16), q_spec
    else:
        dq_shape, dq_spec = acc_shape, acc_spec
    grads, dq = pl.pallas_call(
        functools.partial(attend_back_kernel, n, acc is not None, finish),
        grid_spec=pltpu.PrefetchScalarGridSpec(
            num_scalar_prefetch=1,
            grid=(seqs,),
            in_specs=in_specs,
            out_specs=[
                pl.BlockSpec((n, 1, span, kv_width), lambda b, *_: (0, b, 0, 0)),
                dq_spec,
            ],
            scratch_shapes=[
                pltpu.VMEM((2, n, span, kv_width), bf16),
                pltpu.SemaphoreType.DMA((2, n)),
                pltpu.VMEM((128, 2 * span), f32),
                pltpu.VMEM((2 * span, 256), bf16),
                pltpu.VMEM((2 * span, 256), bf16),
            ],
        ),
        out_shape=[jax.ShapeDtypeStruct((n, seqs, span, kv_width), bf16), dq_shape],
        compiler_params=params(1),
        cost_estimate=pl.CostEstimate(
            flops=10 * 4 * seqs * span * width * span * n,
            bytes_accessed=4 * seqs * (span * width * 4 + span * n * width),
            transcendentals=seqs * span * width // 64 * span * n,
        ),
    )(jnp.concatenate([info, bases]), *args)
    return [grads[i] for i in range(n)] + [dq]


def unproject_kernel(
    head_dim,
    info_ref,
    grad_ref,
    raw_ref,
    scale_ref,
    gain_ref,
    cos_ref,
    sa_ref,
    sb_ref,
    out_ref,
    sum_ref,
):
    @pl.when(pl.program_id(0) == 0)
    def _():
        sum_ref[...] = jnp.zeros(sum_ref.shape, f32)

    alive = info_ref[0] < info_ref[1 + pl.program_id(0)]

    @pl.when(jnp.logical_not(alive))
    def _():
        out_ref[...] = jnp.zeros(out_ref.shape, out_ref.dtype)

    @pl.when(alive)
    def _():
        scale = scale_ref[:, :1]
        mean_matrix = group_matrix(head_dim, 1.0 / head_dim)
        normed = raw_ref.shape[1]
        for slab in range(normed // 128):
            lanes = slice(128 * slab, 128 * slab + 128)
            raw = raw_ref[:, lanes].astype(f32)
            inverse = lax.rsqrt(group_sum(raw * raw, mean_matrix) + norm_eps)
            unit = raw * inverse
            turned = turn_back(grad_ref[:, lanes].astype(f32), cos_ref, sa_ref, sb_ref)
            sum_ref[...] += jnp.broadcast_to(
                jnp.sum(turned * unit, axis=0, keepdims=True), sum_ref.shape
            )
            inner = turned * gain_ref[...]
            mean = group_sum(inner * unit, mean_matrix)
            out_ref[:, lanes] = (inverse * (inner - unit * mean) * scale).astype(bf16)
        if normed < grad_ref.shape[1]:
            out_ref[:, normed:] = (grad_ref[:, normed:].astype(f32) * scale).astype(bf16)


def unproject(info, grad, raw, scale, gain, tables, head_dim):
    rows, width = grad.shape
    span = tables[0].shape[0]
    row_block = lambda a: pl.BlockSpec((span, a.shape[1]), lambda i, *_: (i, 0))
    fixed = lambda a: pl.BlockSpec(a.shape, lambda i, *_: (0,) * a.ndim)
    return pl.pallas_call(
        functools.partial(unproject_kernel, head_dim),
        grid_spec=pltpu.PrefetchScalarGridSpec(
            num_scalar_prefetch=1,
            grid=(rows // span,),
            in_specs=[row_block(a) for a in (grad, raw, scale)]
            + [fixed(a) for a in (gain, *tables)],
            out_specs=[row_block(grad), pl.BlockSpec((8, 128), lambda i, *_: (0, 0))],
        ),
        out_shape=[
            jax.ShapeDtypeStruct((rows, width), bf16),
            jax.ShapeDtypeStruct((8, 128), f32),
        ],
        compiler_params=params(1),
        cost_estimate=pl.CostEstimate(
            flops=8 * 128 * rows * width,
            bytes_accessed=6 * rows * width,
            transcendentals=rows * width,
        ),
    )(info, grad, raw, scale, gain, *tables)


def feed_kernel(
    grid,
    span,
    split,
    info_ref,
    place_ref,
    tok_ref,
    heads_ref,
    cot_ref,
    *rest,
):
    pieces, rest = rest[:8], rest[8:]
    out_ref, hidden_ref, mid_ref, dgu_ref, dmid_ref, dheads_ref, *rest = rest
    w_out, w_gu, w_down, out_sems, gu_sems, down_sems = rest
    a, b = split

    @pl.when(pl.program_id(0) == 0)
    def _():
        copies = (
            loads(grid, place_ref, pieces, w_out, out_sems, (0, a))
            + loads(grid, place_ref, pieces, w_gu, gu_sems, (2 * a, 2 * a + b))
            + loads(grid, place_ref, pieces, w_down, down_sems, (a, 2 * a))
        )
        for copy in copies:
            copy.start()
        for copy in copies:
            copy.wait()

    rows = tok_ref.shape[0]
    middle = tok_ref[...].astype(f32) + mm(heads_ref[...], w_out[...], NT)
    middle_low = middle.astype(bf16)
    mid_ref[...] = middle_low
    scale = lax.rsqrt(jnp.mean(middle * middle, axis=-1, keepdims=True) + norm_eps)
    gate_up = mm(middle_low, w_gu[...]) * scale
    half = gate_up.shape[1] // 2
    gate, up = gate_up[:, :half], gate_up[:, half:]
    sig = 1.0 / (1.0 + jnp.exp(-gate))
    silu = gate * sig
    hidden = silu * up
    hidden_low = hidden.astype(bf16)
    out_ref[...] = (middle + mm(hidden_low, w_down[...], NT)).astype(bf16)

    first = pl.program_id(0) * (rows // span)
    count = rows // span
    longest = info_ref[1 + first]
    for k in range(1, count):
        longest = jnp.maximum(longest, info_ref[1 + first + k])
    alive = info_ref[0] < longest

    @pl.when(alive)
    def _():
        position = lax.broadcasted_iota(jnp.int32, (span, 1), 0) + info_ref[0]
        valid = jnp.concatenate(
            [(position < info_ref[1 + first + k]).astype(f32) for k in range(count)], axis=0
        )
        hidden_ref[...] = (hidden * valid).astype(bf16)
        cot = cot_ref[...].astype(f32) * valid
        grad_hidden = mm(cot.astype(bf16), w_down[...])
        grad_gate = grad_hidden * up * (sig * (1.0 + gate * (1.0 - sig))) * scale
        grad_up = grad_hidden * silu * scale
        grad_gu = jnp.concatenate([grad_gate.astype(bf16), grad_up.astype(bf16)], axis=1)
        dgu_ref[...] = grad_gu
        back = mm(grad_gu, w_gu[...], NT)
        unit = middle * scale
        grad_mid = cot + back - unit * jnp.mean(back * unit, axis=-1, keepdims=True)
        grad_mid = grad_mid.astype(bf16)
        dmid_ref[...] = grad_mid
        dheads_ref[...] = mm(grad_mid, w_out[...]).astype(bf16)

    @pl.when(jnp.logical_not(alive))
    def _():
        for ref in (hidden_ref, dgu_ref, dmid_ref, dheads_ref):
            ref[...] = jnp.zeros(ref.shape, ref.dtype)


def feed(grid, info, tokens, heads, cotangent, pieces, split, span):
    rows, width = tokens.shape
    a, b = split
    tile = max(span, min(256, rows))
    block = lambda n: pl.BlockSpec((tile, n), lambda i, *_: (i, 0))
    shape = lambda n: jax.ShapeDtypeStruct((rows, n), bf16)
    n = n_loads(grid)
    outs = (width, a, width, b, width, a)
    macs = width * (2 * a + b)
    return pl.pallas_call(
        functools.partial(feed_kernel, grid, span, split),
        grid_spec=pltpu.PrefetchScalarGridSpec(
            num_scalar_prefetch=2,
            grid=(rows // tile,),
            in_specs=[block(width), block(a), block(width)] + [any_spec] * 8,
            out_specs=[block(n) for n in outs],
            scratch_shapes=[
                pltpu.VMEM((width, a), bf16),
                pltpu.VMEM((width, b), bf16),
                pltpu.VMEM((width, a), bf16),
                pltpu.SemaphoreType.DMA((n,)),
                pltpu.SemaphoreType.DMA((n,)),
                pltpu.SemaphoreType.DMA((n,)),
            ],
        ),
        out_shape=[shape(n) for n in outs],
        compiler_params=params(1),
        cost_estimate=pl.CostEstimate(
            flops=6 * rows * macs,
            bytes_accessed=2 * (rows * (sum(outs) + 2 * width + a) + macs),
            transcendentals=rows * a,
        ),
    )(info, grid.place, tokens, heads, cotangent, *pieces)


def load_all(copies):
    for copy in copies:
        copy.start()
    for copy in copies:
        copy.wait()


def query_back_kernel(grid, info_ref, place_ref, grad_ref, *rest):
    pieces, (out_ref, weight, sems) = rest[:2], rest[2:]

    @pl.when(pl.program_id(0) == 0)
    def _():
        load_all(loads(grid, place_ref, pieces, weight, sems))

    @pl.when(info_ref[0] < info_ref[1 + pl.program_id(0)])
    def _():
        out_ref[...] = mm(grad_ref[...], weight[...], NT)


def query_back(grid, info, grad, pieces, width, span):
    rows, inner = grad.shape
    return pl.pallas_call(
        functools.partial(query_back_kernel, grid),
        grid_spec=pltpu.PrefetchScalarGridSpec(
            num_scalar_prefetch=2,
            grid=(rows // span,),
            in_specs=[pl.BlockSpec((span, inner), lambda i, *_: (i, 0))] + [any_spec] * 2,
            out_specs=pl.BlockSpec((span, width), lambda i, *_: (i, 0)),
            scratch_shapes=[
                pltpu.VMEM((width, inner), bf16),
                pltpu.SemaphoreType.DMA((n_loads(grid),)),
            ],
        ),
        out_shape=jax.ShapeDtypeStruct((rows, width), f32),
        compiler_params=params(1),
        cost_estimate=pl.CostEstimate(
            flops=2 * rows * width * inner,
            bytes_accessed=2 * (rows * (2 * width + inner) + width * inner),
            transcendentals=0,
        ),
    )(info, grid.place, grad, *pieces)


def last_kernel(grid, info_ref, place_ref, tok_ref, grad_ref, back_ref, dmid_ref, scale_ref, *rest):
    pieces, (out_ref, weight, sems) = rest[:2], rest[2:]

    @pl.when(pl.program_id(0) == 0)
    def _():
        load_all(loads(grid, place_ref, pieces, weight, sems))

    alive = info_ref[0] < info_ref[1 + pl.program_id(0)]

    @pl.when(alive)
    def _():
        back = back_ref[...] + mm(grad_ref[...], weight[...], NT)
        unit = tok_ref[...].astype(f32) * scale_ref[:, :1]
        grad = dmid_ref[...].astype(f32) + back
        grad = grad - unit * jnp.mean(back * unit, axis=-1, keepdims=True)
        out_ref[...] = grad.astype(bf16)

    @pl.when(jnp.logical_not(alive))
    def _():
        out_ref[...] = jnp.zeros(out_ref.shape, out_ref.dtype)


def last(grid, info, tokens, grad_kv, back, grad_mid, scale, pieces, span):
    rows, width = tokens.shape
    block = lambda a: pl.BlockSpec((span, a.shape[1]), lambda i, *_: (i, 0))
    inner = grad_kv.shape[1]
    args = (tokens, grad_kv, back, grad_mid, scale)
    return pl.pallas_call(
        functools.partial(last_kernel, grid),
        grid_spec=pltpu.PrefetchScalarGridSpec(
            num_scalar_prefetch=2,
            grid=(rows // span,),
            in_specs=[block(a) for a in args] + [any_spec] * 2,
            out_specs=block(tokens),
            scratch_shapes=[
                pltpu.VMEM((width, inner), bf16),
                pltpu.SemaphoreType.DMA((n_loads(grid),)),
            ],
        ),
        out_shape=jax.ShapeDtypeStruct(tokens.shape, bf16),
        compiler_params=params(1),
        cost_estimate=pl.CostEstimate(
            flops=2 * rows * width * inner,
            bytes_accessed=2 * (rows * (5 * width + inner) + width * inner),
            transcendentals=0,
        ),
    )(info, grid.place, *args, *pieces)


def weight_kernel(grid, shard, span, n_pairs, place_ref, info_ref, *refs):
    lefts, rights = refs[:n_pairs], refs[n_pairs : 2 * n_pairs]
    mine_ref, theirs_ref, acc = refs[2 * n_pairs :]
    core = place_ref[2]
    middle = grid.depth // 2
    n_seqs = lefts[0].shape[0] // span
    shortest = info_ref[1]
    for seq in range(1, n_seqs):
        shortest = jnp.minimum(shortest, info_ref[1 + seq])
    all_alive = info_ref[0] < shortest
    column = 0
    for left, right in zip(lefts, rights):
        width = right.shape[1]

        @pl.when(all_alive)
        def _(left=left, right=right, width=width):
            acc[:, :width] = mm(left[...], right[...], TN)

        @pl.when(jnp.logical_not(all_alive))
        def _(left=left, right=right, width=width):
            acc[:, :width] = jnp.zeros((acc.shape[0], width), f32)
            for seq in range(n_seqs):
                rows = slice(seq * span, (seq + 1) * span)

                @pl.when(info_ref[0] < info_ref[1 + seq])
                def _(rows=rows):
                    acc[:, :width] += mm(left[rows, :], right[rows, :], TN)

        for level in range(grid.depth):
            half, at = level // middle, level % middle
            for whose, ref in ((core, mine_ref), (1 - core, theirs_ref)):
                start = pl.multiple_of((level * 2 + whose) * shard, shard)
                ref[half, 0, at, :, column : column + width] = acc[
                    pl.ds(start, shard), :width
                ].astype(bf16)
        column += width


def weight_grad(grid, info, span, *pairs):
    lefts, rights = [p[0] for p in pairs], [p[1] for p in pairs]
    rows, features = lefts[0].shape
    widths = [r.shape[1] for r in rights]
    total = sum(widths)
    part = features // grid.rows
    shard = part // grid.seqs
    middle = grid.depth // 2
    shape = jax.ShapeDtypeStruct((2, grid.rows, middle, shard, total), bf16)
    piece = pl.BlockSpec((2, 1, middle, shard, total), lambda i, *_: (0, i, 0, 0, 0))
    return pl.pallas_call(
        functools.partial(weight_kernel, grid, shard, span, len(pairs)),
        grid_spec=pltpu.PrefetchScalarGridSpec(
            num_scalar_prefetch=2,
            grid=(grid.rows,),
            in_specs=[pl.BlockSpec((rows, part), lambda i, place, info: (0, place[0] ^ i))]
            * len(pairs)
            + [pl.BlockSpec(r.shape, lambda i, *_: (0, 0)) for r in rights],
            out_specs=[piece, piece],
            scratch_shapes=[pltpu.VMEM((part, max(widths)), f32)],
        ),
        out_shape=[shape, shape],
        compiler_params=params(1),
        cost_estimate=pl.CostEstimate(
            flops=2 * rows * features * total,
            bytes_accessed=2 * (rows * (features * len(pairs) + total) + features * total),
            transcendentals=0,
        ),
    )(grid.place, info, *lefts, *rights)


def shards(
    n_rows,
    n_seqs,
    tokens,
    lengths,
    cotangent,
    w_qkv,
    w_out,
    w_gateup,
    w_down,
    norm_attn,
    norm_ffn,
    q_gain,
    k_gain,
):
    grid = Grid(n_rows, n_seqs)
    seq_count, span_len, model_width = tokens.shape
    row_count = seq_count * span_len
    head_dim = q_gain.shape[0]
    half_dim = head_dim // 2
    query_width = w_out.shape[1]
    kv_width = (w_qkv.shape[1] - query_width) // 2
    log2_scale = math.log2(math.e) * head_dim ** (-0.5)

    offset = (grid.seq * span_len).astype(jnp.int32)
    positions = offset + jnp.arange(span_len, dtype=jnp.int32)
    inverse = theta_base ** (-jnp.arange(half_dim, dtype=f32) * 2.0 / head_dim)
    angles = positions.astype(f32)[:, None] * inverse[None, :]
    cosine, sine = jnp.cos(angles), jnp.sin(angles)
    nothing = jnp.zeros_like(sine)
    tables = (
        jnp.concatenate([cosine] * 4, axis=1),
        jnp.concatenate([-sine, nothing] * 2, axis=1),
        jnp.concatenate([nothing, sine] * 2, axis=1),
    )
    q_gain_f = jnp.concatenate([q_gain.astype(f32)] * 2)[None, :]
    k_gain_f = jnp.concatenate([k_gain.astype(f32)] * 2)[None, :]
    info = jnp.concatenate([offset[None], lengths])

    attn_gain = norm_attn.astype(f32)[:, None]
    ffn_gain = norm_ffn.astype(f32)[:, None]
    qkv_shard = (w_qkv.astype(f32) * attn_gain).astype(bf16)
    gateup_shard = (w_gateup.astype(f32) * ffn_gain).astype(bf16)

    order = Order()
    depth = grid.depth
    kv_steps = grid.ring(qkv_shard[:, query_width:])
    kv_own, kv_came = grid.spread(kv_steps)
    q_steps = grid.ring(
        qkv_shard[:, :query_width], [[], [kv_steps[2]]] + [[kv_steps[-1]]] * (depth - 3)
    )
    feed_steps = grid.ring(
        jnp.concatenate([w_out, w_down, gateup_shard], axis=1),
        [[kv_steps[1]], kv_came[0]] + [kv_came[-1]] * (depth - 3),
    )
    kv_pieces = grid.with_partner(kv_own, True)
    q_own, q_came = grid.spread(q_steps, [kv_came[-1]])
    q_pieces = grid.with_partner(q_own, True)
    feed_own, feed_came = grid.spread(feed_steps, [q_came[-1]])

    rows_in = tokens.reshape(row_count, model_width)
    kv, k_raw, scale1 = project(grid, rows_in, kv_pieces, k_gain_f, tables, kv_width, head_dim)
    order.leave(kv)
    kv = kv.reshape(seq_count, span_len, 2 * kv_width)
    q, q_raw = project(
        grid,
        order.enter(rows_in),
        q_pieces,
        q_gain_f * log2_scale,
        tables,
        query_width,
        head_dim,
        scale1,
    )
    order.leave(q)
    order.pin(*feed_came[0])
    feed_held = [grid.partner(order.late(feed_own[k])) for k in (0, 2)]
    q = q.reshape(seq_count, span_len, query_width)

    reach = [kv]
    for step in range(1, depth):
        held = reach[-1] if step == 1 else order.late(reach[-1])
        reach.append(grid.up(held))
    chunks, bases = [], []
    for step in range(depth):
        level = grid.level - step
        start = jnp.stack([level * 2 + grid.core, level * 2 + 1 - grid.core]) * span_len
        bases.append(jnp.where(level >= 0, start, -1).astype(jnp.int32))
    chunks = [(own, grid.partner(own)) for own in reach[:-1]]
    near = [c for pair in chunks for c in pair]
    acc = attend(info, jnp.concatenate(bases[:-1]), order.enter(q), near, None, False)
    order.leave(acc)
    feed_found = [grid.partner(order.late(feed_own[k])) for k in (1, 3)]
    order.pin(*feed_came[-1], *feed_held)
    feed_pieces = feed_own + [feed_held[0], feed_found[0], feed_held[1], feed_found[1]]
    farthest = order.late(reach[-1])
    chunks.append((farthest, grid.partner(farthest)))
    heads, logs = attend(info, bases[-1], order.enter(q), list(chunks[-1]), acc, True)
    order.leave(heads)
    attended = heads.reshape(row_count, query_width)

    flat_cot = cotangent.reshape(row_count, model_width)
    output, hidden, middle, grad_gu, grad_mid, grad_heads = feed(
        grid,
        info,
        rows_in,
        attended,
        flat_cot,
        feed_pieces,
        (query_width, w_gateup.shape[1]),
        span_len,
    )
    order.leave(hidden)
    grad_heads = grad_heads.reshape(seq_count, span_len, query_width)

    def advance(*sums):
        for each in sums:
            order.pin(*each.land())
            order.pin(*each.go())

    kv_flight = []

    def kv_hop(own, other):
        kv_flight[:] = [order.late(came) for came in kv_flight]
        order.pin(other, *kv_flight)
        here = own.astype(f32) + other.astype(f32)
        for came in kv_flight:
            here = here + came.astype(f32)
        sent = order.late(here.astype(bf16))
        order.pin(sent)
        kv_flight[:] = [grid.down(sent)]

    feed_sum = Sum(
        grid,
        order,
        weight_grad(grid, info, span_len, (flat_cot, hidden), (middle, grad_gu)),
    )
    order.leave(feed_sum.theirs)
    advance(feed_sum)

    split = max(1, depth // 2)
    far = [c for pair in chunks[split:] for c in pair]
    near = [c for pair in chunks[:split] for c in pair]
    *far_grads, acc_q = attend_back(
        info,
        jnp.concatenate(bases[split:]),
        order.enter(q),
        grad_heads,
        heads,
        logs,
        far,
        None,
        False,
    )
    order.leave(acc_q)
    far_grads = [far_grads[2 * k : 2 * k + 2] for k in range(depth - split)]
    crossed = [grid.partner(other) for _, other in far_grads]
    kv_hop(far_grads[-1][0], crossed[-1])
    advance(feed_sum)
    *near_grads, grad_q = attend_back(
        info,
        jnp.concatenate(bases[:split]),
        order.enter(q),
        grad_heads,
        heads,
        logs,
        near,
        acc_q,
        True,
    )
    order.leave(grad_q)
    near_grads = [near_grads[2 * k : 2 * k + 2] for k in range(split)]
    crossed = [grid.partner(order.late(other)) for _, other in near_grads] + crossed
    all_grads = near_grads + far_grads
    for step in reversed(range(split, depth - 1)):
        kv_hop(all_grads[step][0], crossed[step])
    advance(feed_sum)
    grad_pq, gq = unproject(
        info,
        order.enter(grad_q.reshape(row_count, query_width)),
        q_raw,
        scale1,
        q_gain_f,
        tables,
        head_dim,
    )
    order.leave(grad_pq)
    square_sum = Sum(
        grid,
        order,
        weight_grad(
            grid, info, span_len, (rows_in, order.enter(grad_pq)), (grad_mid, attended)
        ),
    )
    order.leave(square_sum.theirs)
    for step in reversed(range(1, split)):
        kv_hop(all_grads[step][0], crossed[step])
    advance(feed_sum, square_sum)
    back_q = query_back(grid, info, order.enter(grad_pq), q_pieces, model_width, span_len)
    order.leave(back_q)

    kv_flight = [order.late(came) for came in kv_flight]
    order.pin(*kv_flight)
    advance(feed_sum, square_sum)
    grad_kv = all_grads[0][0].astype(f32) + crossed[0].astype(f32)
    for came in kv_flight:
        grad_kv = grad_kv + came.astype(f32)
    grad_kv = grad_kv.astype(bf16).reshape(row_count, 2 * kv_width)
    grad_pkv, gk = unproject(
        info, order.enter(grad_kv), k_raw, scale1, k_gain_f, tables, head_dim
    )
    order.leave(grad_pkv)
    kv_sum = Sum(
        grid, order, weight_grad(grid, info, span_len, (rows_in, order.enter(grad_pkv)))
    )
    order.leave(kv_sum.theirs)
    advance(feed_sum, square_sum, kv_sum)
    grad_tokens = last(
        grid,
        info,
        rows_in,
        order.enter(grad_pkv),
        back_q,
        grad_mid,
        scale1,
        kv_pieces,
        span_len,
    )
    order.leave(grad_tokens)
    gains = grid.everywhere(jnp.concatenate([gq[:1], gk[:1]], axis=0))
    gains = gains[:, :head_dim] + gains[:, head_dim:]
    kv_total, square_total, feed_total = kv_sum.finish(), square_sum.finish(), feed_sum.finish()
    sum_qkv = jnp.concatenate([square_total[:, :query_width], kv_total], axis=1)
    sum_out = square_total[:, query_width:]
    sum_down, sum_gateup = feed_total[:, :query_width], feed_total[:, query_width:]
    return (
        output.reshape(tokens.shape),
        grad_tokens.reshape(tokens.shape),
        sum_qkv * attn_gain,
        sum_out,
        sum_gateup * ffn_gain,
        sum_down,
        jnp.sum(sum_qkv * w_qkv.astype(f32), axis=1),
        jnp.sum(sum_gateup * w_gateup.astype(f32), axis=1),
        gains[0],
        gains[1],
    )


def solution(mesh):
    rows = P("row", "seq", None)
    weight = P(both, None)
    vector = P(both)
    return jax.shard_map(
        functools.partial(shards, mesh.shape["row"], mesh.shape["seq"]),
        mesh=mesh,
        in_specs=(rows, P("row"), rows, weight, weight, weight, weight, vector, vector, P(), P()),
        out_specs=(rows, rows, weight, weight, weight, weight, vector, vector, P(), P()),
        check_vma=False,
    )
```

profile of v0, /device:TPU:0, one launch (start us, length us, event | category | flops | bytes accessed | tf_op | source)
XLA Modules:
  0.0 579.8 jit_solution(1765934639461726564)
XLA Ops:
  65.2 12.5 %collective-permute-done.16 = bf16[64,4096]{1,0:T(8,128)(2,1)} collective-permute-done((bf16[64,4096]{1,0:T(8,128)(2,1)}, bf16[64,4096]{1,0:T(8,128)(2,1)}, u32[]{:S(2)}, u32[]{:S(2)}) %collective-permute-start.16) | collective-permute-done | bytes 524320 | tf_op jit(solution)/shard_map/ppermute | solution.py:87
  77.7 9.3 %shard_map.186 = (bf16[1024,512]{1,0:T(8,128)(2,1)}, bf16[1024,256]{1,0:T(8,128)(2,1)}, f32[1024,128]{1,0:T(8,128)}) custom-call(s32[3]{0:T(128)} %pad_add_fusion.1.place_ref, bf16[1024,2048]{1,0:T(8,128)(2,1)} %bitcast.207, bf16[4,2,2,64,512]{4,3,2,1,0:T(8,128)(2,1)} %copy-done, bf16[4,2,2,64,512]{4,3,2,1,0:T(8,128)(2,1)} %collective-permute-done.7.rest_1_, ...), custom_call_target="tpu_custom_call" | custom-call | flops 4294967296 | bytes 8388608 | tf_op jit(solution)/shard_map/pallas_call | solution.py:327
  93.0 13.3 %shard_map.187 = (bf16[1024,1024]{1,0:T(8,128)(2,1)}, bf16[1024,1024]{1,0:T(8,128)(2,1)}) custom-call(s32[3]{0:T(128)} %pad_add_fusion.1.place_ref, bf16[1024,2048]{1,0:T(8,128)(2,1)} %bitcast.208, bf16[4,2,2,64,1024]{4,3,2,1,0:T(8,128)(2,1)} %copy-done.9, bf16[4,2,2,64,1024]{4,3,2,1,0:T(8,128)(2,1)} %collective-permute-done.15.rest_1_, ...), custom_call_target="tpu_custom_call" | custom-call | flops 8589934592 | bytes 12582912 | tf_op jit(solution)/shard_map/pallas_call | solution.py:327
  126.1 19.0 %collective-permute-done.24.refs_4_.refs_0_ = bf16[4,256,512]{2,1,0:T(8,128)(2,1)S(1)} collective-permute-done((bf16[4,256,512]{2,1,0:T(8,128)(2,1)S(1)}, bf16[4,256,512]{2,1,0:T(8,128)(2,1)S(1)}, u32[]{:S(2)}, u32[]{:S(2)}) %collective-permute-start.24) | collective-permute-done | bytes 1048608 | tf_op jit(solution)/shard_map/ppermute | solution.py:87
  156.3 16.9 %shard_map.188.refs_2_ = f32[4,4,512,256]{3,2,1,0:T(8,128)} custom-call(s32[11]{0:T(128)} %concatenate.94.info_ref, bf16[4,256,1024]{2,1,0:T(8,128)(2,1)} %bitcast.236, bf16[4,256,512]{2,1,0:T(8,128)(2,1)} %bitcast.232, bf16[4,256,512]{2,1,0:T(8,128)(2,1)} %copy-done.33, bf16[4,256,512]{2,1,0:T(8,128)(2,1)} %copy-done.32, bf16[4,256,512]{2,1,0:T(8,128)(2,1)} %copy-done.34, ...), custom_call_target="tpu_custom_call" | custom-call | flops 25769803776 | bytes 25165824 | tf_op jit(solution)/shard_map/pallas_call | solution.py:502
  173.2 24.3 %collective-permute-done.27.rest_3_ = bf16[2,2,64,4096]{3,2,1,0:T(8,128)(2,1)} collective-permute-done((bf16[2,2,64,4096]{3,2,1,0:T(8,128)(2,1)}, bf16[2,2,64,4096]{3,2,1,0:T(8,128)(2,1)}, u32[]{:S(2)}, u32[]{:S(2)}) %collective-permute-start.27) | collective-permute-done | bytes 2097184 | tf_op jit(solution)/shard_map/ppermute | solution.py:87
  204.8 8.0 %shard_map.189 = (bf16[4,256,1024]{2,1,0:T(8,128)(2,1)}, bf16[4,256,1024]{2,1,0:T(8,128)(2,1)}) custom-call(s32[7]{0:T(128)} %pad_add_fusion.2.info_ref, bf16[4,256,1024]{2,1,0:T(8,128)(2,1)} %bitcast.237, bf16[4,256,512]{2,1,0:T(8,128)(2,1)} %copy-done.37, bf16[4,256,512]{2,1,0:T(8,128)(2,1)} %collective-permute-done.31.refs_1_.refs_3_, ...), custom_call_target="tpu_custom_call" | custom-call | flops 8589934592 | bytes 16777216 | tf_op jit(solution)/shard_map/pallas_call | solution.py:502
  212.8 50.7 %shard_map.190 = (bf16[1024,2048]{1,0:T(8,128)(2,1)}, bf16[1024,1024]{1,0:T(8,128)(2,1)}, bf16[1024,2048]{1,0:T(8,128)(2,1)}, bf16[1024,2048]{1,0:T(8,128)(2,1)}...) custom-call(s32[5]{0:T(128)} %pad_add_fusion.info_ref, s32[3]{0:T(128)} %pad_add_fusion.1.place_ref, ...), custom_call_target="tpu_custom_call" | custom-call | flops 51539607552 | bytes 48234496 | tf_op jit(solution)/shard_map/pallas_call | solution.py:808
  263.6 22.0 %shard_map.191 = (bf16[2,4,2,64,3072]{4,3,2,1,0:T(8,128)(2,1)}, bf16[2,4,2,64,3072]{4,3,2,1,0:T(8,128)(2,1)}) custom-call(s32[3]{0:T(128)} %pad_add_fusion.1.place_ref, s32[5]{0:T(128)} %pad_add_fusion.info_ref, bf16[1024,2048]{1,0:T(8,128)(2,1)} %bitcast.230, bf16[1024,2048]{1,0:T(8,128)(2,1)} %get-tuple-element.141.refs_1_, ...), custom_call_target="tpu_custom_call" | custom-call | flops 12884901888 | bytes 27262976 | tf_op jit(solution)/shard_map/pallas_call | solution.py:974
  286.2 10.9 %shard_map.192 = (bf16[4,4,256,512]{3,2,1,0:T(8,128)(2,1)}, f32[4,4,128,512]{3,2,1,0:T(8,128)}) custom-call(s32[9]{0:T(128)} %get-tuple-element.254.info_ref, bf16[4,256,1024]{2,1,0:T(8,128)(2,1)} %bitcast.238, bf16[4,256,1024]{2,1,0:T(8,128)(2,1)} %bitcast.242, bf16[4,256,1024]{2,1,0:T(8,128)(2,1)} %get-tuple-element.137.o_ref, ...), custom_call_target="tpu_custom_call" | custom-call | flops 42949672960 | bytes 33554432 | tf_op jit(solution)/shard_map/pallas_call | solution.py:624
  315.8 26.9 %shard_map.193 = (bf16[4,4,256,512]{3,2,1,0:T(8,128)(2,1)}, bf16[4,256,1024]{2,1,0:T(8,128)(2,1)}) custom-call(s32[9]{0:T(128)} %get-tuple-element.253.info_ref, bf16[4,256,1024]{2,1,0:T(8,128)(2,1)} %bitcast.239, bf16[4,256,1024]{2,1,0:T(8,128)(2,1)} %bitcast.243, bf16[4,256,1024]{2,1,0:T(8,128)(2,1)} %get-tuple-element.137.o_ref, ...), custom_call_target="tpu_custom_call" | custom-call | flops 42949672960 | bytes 33554432 | tf_op jit(solution)/shard_map/pallas_call | solution.py:624
  356.8 9.8 %collective-permute-start.44 = (bf16[1,2,64,3072]{3,2,1,0:T(8,128)(2,1)}, bf16[1,2,64,3072]{3,2,1,0:T(8,128)(2,1)}, u32[]{:S(2)}, u32[]{:S(2)}) collective-permute-start(bf16[1,2,64,3072]{3,2,1,0:T(8,128)(2,1)} %fusion.8), channel_id=1, source_target_pairs={{0,8},{1,9},{2,10},{3,11},{4,12},{5,13},{6,14},{7,15},{8,0},{9,1},... | collective-permute-start | bytes 2359304 | tf_op jit(solution)/shard_map/ppermute | solution.py:87
  369.0 8.6 %shard_map.194 = (bf16[1024,1024]{1,0:T(8,128)(2,1)}, f32[8,128]{1,0:T(8,128)}) custom-call(s32[5]{0:T(128)} %pad_add_fusion.info_ref, bf16[1024,1024]{1,0:T(8,128)(2,1)} %bitcast.214, bf16[1024,1024]{1,0:T(8,128)(2,1)} %get-tuple-element.168.raw_ref, f32[1024,128]{1,0:T(8,128)} %get-tuple-element.123.rest_6_.scale_ref, ...), custom_call_target="tpu_custom_call" | custom-call | flops 1073741824 | bytes 6291456 | tf_op jit(solution)/shard_map/pallas_call | solution.py:702
  378.3 16.1 %shard_map.195 = (bf16[2,4,2,64,2048]{4,3,2,1,0:T(8,128)(2,1)}, bf16[2,4,2,64,2048]{4,3,2,1,0:T(8,128)(2,1)}) custom-call(s32[3]{0:T(128)} %pad_add_fusion.1.place_ref, s32[5]{0:T(128)} %pad_add_fusion.info_ref, bf16[1024,2048]{1,0:T(8,128)(2,1)} %bitcast.210, bf16[1024,2048]{1,0:T(8,128)(2,1)} %get-tuple-element.162.refs_1_.dmid_ref, ...), custom_call_target="tpu_custom_call" | custom-call | flops 8589934592 | bytes 20971520 | tf_op jit(solution)/shard_map/pallas_call | solution.py:974
  405.4 6.6 %collective-permute-start.46 = (bf16[64,3072]{1,0:T(8,128)(2,1)S(1)}, bf16[64,3072]{1,0:T(8,128)(2,1)S(1)}, u32[]{:S(2)}, u32[]{:S(2)}) collective-permute-start(bf16[64,3072]{1,0:T(8,128)(2,1)S(1)} %fusion.41), channel_id=1, source_target_pairs={{0,2},{1,3},{2,4},{3,5},{4,6},{5,7},{6,0},{7,1},{8,10},{9,11},{10,... | collective-permute-start | bytes 1179656 | tf_op jit(solution)/shard_map/ppermute | solution.py:87
  412.0 10.9 %shard_map.196.back_ref = f32[1024,2048]{1,0:T(8,128)} custom-call(s32[5]{0:T(128)} %pad_add_fusion.info_ref, s32[3]{0:T(128)} %pad_add_fusion.1.place_ref, bf16[1024,1024]{1,0:T(8,128)(2,1)} %get-tuple-element.177.refs_2_.grad_ref, bf16[4,2,2,64,1024]{4,3,2,1,0:T(8,128)(2,1)} %copy-done.9, bf16[4,2,2,64,1024]{4,3,2,1,0:T(8,128)(2,1)} %collective-permute-done.15.rest_1_), custom_call_target="tpu_custom_call" | custom-call | flops 4294967296 | bytes 14680064 | tf_op jit(solution)/shard_map/pallas_call | solution.py:855
  422.9 7.5 %collective-permute-done.43 = bf16[4,256,512]{2,1,0:T(8,128)(2,1)} collective-permute-done((bf16[4,256,512]{2,1,0:T(8,128)(2,1)}, bf16[4,256,512]{2,1,0:T(8,128)(2,1)}, u32[]{:S(2)}, u32[]{:S(2)}) %collective-permute-start.43) | collective-permute-done | bytes 1048608 | tf_op jit(solution)/shard_map/ppermute | solution.py:87
  433.7 31.8 %collective-permute-done.46 = bf16[64,3072]{1,0:T(8,128)(2,1)S(1)} collective-permute-done((bf16[64,3072]{1,0:T(8,128)(2,1)S(1)}, bf16[64,3072]{1,0:T(8,128)(2,1)S(1)}, u32[]{:S(2)}, u32[]{:S(2)}) %collective-permute-start.46) | collective-permute-done | bytes 393248 | tf_op jit(solution)/shard_map/ppermute | solution.py:87
  481.1 6.9 %shard_map.198 = (bf16[2,4,2,64,512]{4,3,2,1,0:T(8,128)(2,1)}, bf16[2,4,2,64,512]{4,3,2,1,0:T(8,128)(2,1)}) custom-call(s32[3]{0:T(128)} %pad_add_fusion.1.place_ref, s32[5]{0:T(128)} %pad_add_fusion.info_ref, bf16[1024,2048]{1,0:T(8,128)(2,1)} %bitcast.211, bf16[1024,512]{1,0:T(8,128)(2,1)} %get-tuple-element.196.refs_1_.grad_ref), custom_call_target="tpu_custom_call" | custom-call | flops 2147483648 | bytes 7340032 | tf_op jit(solution)/shard_map/pallas_call | solution.py:974
  489.6 8.2 %collective-permute-done.65 = f32[2,128]{1,0:T(2,128)S(1)} collective-permute-done((f32[2,128]{1,0:T(2,128)S(1)}, f32[2,128]{1,0:T(2,128)S(1)}, u32[]{:S(2)}, u32[]{:S(2)}) %collective-permute-start.65) | collective-permute-done | bytes 1056 | tf_op jit(solution)/shard_map/ppermute | solution.py:87
  503.5 13.1 %shard_map.199 = bf16[1024,2048]{1,0:T(8,128)(2,1)} custom-call(s32[5]{0:T(128)} %pad_add_fusion.info_ref, s32[3]{0:T(128)} %pad_add_fusion.1.place_ref, bf16[1024,2048]{1,0:T(8,128)(2,1)} %bitcast.212, bf16[1024,512]{1,0:T(8,128)(2,1)} %get-tuple-element.196.refs_1_.grad_ref, f32[1024,2048]{1,0:T(8,128)} %shard_map.196.back_ref, ...), custom_call_target="tpu_custom_call" | custom-call | flops 2147483648 | bytes 24117248 | tf_op jit(solution)/shard_map/pallas_call | solution.py:904
  542.4 6.2 %collective-permute-done.52 = bf16[1,2,64,2048]{3,2,1,0:T(8,128)(2,1)S(1)} collective-permute-done((bf16[1,2,64,2048]{3,2,1,0:T(8,128)(2,1)}, bf16[1,2,64,2048]{3,2,1,0:T(8,128)(2,1)S(1)}, u32[]{:S(2)}, u32[]{:S(2)}) %collective-permute-start.52) | collective-permute-done | bytes 524320 | tf_op jit(solution)/shard_map/ppermute | solution.py:87
  553.7 6.2 %collective-permute-done.53 = bf16[64,2048]{1,0:T(8,128)(2,1)S(1)} collective-permute-done((bf16[64,2048]{1,0:T(8,128)(2,1)S(1)}, bf16[64,2048]{1,0:T(8,128)(2,1)S(1)}, u32[]{:S(2)}, u32[]{:S(2)}) %collective-permute-start.53) | collective-permute-done | bytes 262176 | tf_op jit(solution)/shard_map/ppermute | solution.py:87
  561.0 7.7 %collective-permute-done.54 = bf16[64,2048]{1,0:T(8,128)(2,1)S(1)} collective-permute-done((bf16[64,2048]{1,0:T(8,128)(2,1)S(1)}, bf16[64,2048]{1,0:T(8,128)(2,1)S(1)}, u32[]{:S(2)}, u32[]{:S(2)}) %collective-permute-start.54) | collective-permute-done | bytes 262176 | tf_op jit(solution)/shard_map/ppermute | solution.py:87
  (319 shorter events, 224.2 us)
Async XLA Ops:
  57.3 35.7 %collective-permute-start.15 = (bf16[4,2,2,64,1024]{4,3,2,1,0:T(8,128)(2,1)S(1)}, bf16[4,2,2,64,1024]{4,3,2,1,0:T(8,128)(2,1)}, u32[]{:S(2)}, u32[]{:S(2)}) collective-permute-start(bf16[4,2,2,64,1024]{4,3,2,1,0:T(8,128)(2,1)S(1)} %pad_maximum_fusion.rest_0_), channel_id=1, source_target_pairs={{0,1},{1,0},{2,3},{3,2},{4,5},{5,4},{6,7},{7,6},{8,9},{9,8},{10,11... | collective-permute-start | bytes 6291464 | tf_op jit(solution)/shard_map/ppermute | solution.py:87
  93.0 30.4 %collective-permute-start.19 = (bf16[64,4096]{1,0:T(8,128)(2,1)S(1)}, bf16[64,4096]{1,0:T(8,128)(2,1)S(1)}, u32[]{:S(2)}, u32[]{:S(2)}) collective-permute-start(bf16[64,4096]{1,0:T(8,128)(2,1)S(1)} %collective-permute-done.18), channel_id=1, source_target_pairs={{0,2},{1,3},{2,4},{3,5},{4,6},{5,7},{6,0},{7,1},{8,10},{9,11},{10,... | collective-permute-start | bytes 1572872 | tf_op jit(solution)/shard_map/ppermute | solution.py:87
  112.2 32.9 %collective-permute-start.24 = (bf16[4,256,512]{2,1,0:T(8,128)(2,1)S(1)}, bf16[4,256,512]{2,1,0:T(8,128)(2,1)S(1)}, u32[]{:S(2)}, u32[]{:S(2)}) collective-permute-start(bf16[4,256,512]{2,1,0:T(8,128)(2,1)S(1)} %collective-permute-done.22.refs_2_), channel_id=1, source_target_pairs={{0,2},{1,3},{2,4},{3,5},{4,6},{5,7},{8,10},{9,11},{10,12},{11,13},... | collective-permute-start | bytes 3145736 | tf_op jit(solution)/shard_map/ppermute | solution.py:87
  117.7 28.6 %collective-permute-start.17 = (bf16[1,2,64,4096]{3,2,1,0:T(8,128)(2,1)S(1)}, bf16[1,2,64,4096]{3,2,1,0:T(8,128)(2,1)S(1)}, u32[]{:S(2)}, u32[]{:S(2)}) collective-permute-start(bf16[1,2,64,4096]{3,2,1,0:T(8,128)(2,1)S(1)} %maximum_bitcast_fusion), channel_id=1, source_target_pairs={{0,8},{1,9},{2,10},{3,11},{4,12},{5,13},{6,14},{7,15},{8,0},{9,1},... | collective-permute-start | bytes 3145736 | tf_op jit(solution)/shard_map/ppermute | solution.py:87
  146.4 51.1 %collective-permute-start.26 = (bf16[2,2,64,4096]{3,2,1,0:T(8,128)(2,1)S(1)}, bf16[2,2,64,4096]{3,2,1,0:T(8,128)(2,1)}, u32[]{:S(2)}, u32[]{:S(2)}) collective-permute-start(bf16[2,2,64,4096]{3,2,1,0:T(8,128)(2,1)S(1)} %constant_dynamic-update-slice_fusion.4.rest_0_), channel_id=1, source_target_pairs={{0,16},{1,17},{2,18},{3,19},{4,20},{5,21},{6,22},{7,23},{8,24},{9,... | collective-permute-start | bytes 6291464 | tf_op jit(solution)/shard_map/ppermute | solution.py:87
  149.5 48.0 %collective-permute-start.27 = (bf16[2,2,64,4096]{3,2,1,0:T(8,128)(2,1)}, bf16[2,2,64,4096]{3,2,1,0:T(8,128)(2,1)}, u32[]{:S(2)}, u32[]{:S(2)}) collective-permute-start(bf16[2,2,64,4096]{3,2,1,0:T(8,128)(2,1)} %constant_dynamic-update-slice_fusion.6.rest_2_), channel_id=1, source_target_pairs={{0,8},{1,9},{2,10},{3,11},{4,12},{5,13},{6,14},{7,15},{8,0},{9,1},... | collective-permute-start | bytes 6291464 | tf_op jit(solution)/shard_map/ppermute | solution.py:87
  150.0 49.5 %collective-permute-start.28 = (bf16[2,2,64,4096]{3,2,1,0:T(8,128)(2,1)S(1)}, bf16[2,2,64,4096]{3,2,1,0:T(8,128)(2,1)}, u32[]{:S(2)}, u32[]{:S(2)}) collective-permute-start(bf16[2,2,64,4096]{3,2,1,0:T(8,128)(2,1)S(1)} %constant_dynamic-update-slice_fusion.4.rest_0_), channel_id=1, source_target_pairs={{0,1},{1,0},{2,3},{3,2},{4,5},{5,4},{6,7},{7,6},{8,9},{9,8},{10,11... | collective-permute-start | bytes 6291464 | tf_op jit(solution)/shard_map/ppermute | solution.py:87
  150.1 49.4 %collective-permute-start.29 = (bf16[2,2,64,4096]{3,2,1,0:T(8,128)(2,1)}, bf16[2,2,64,4096]{3,2,1,0:T(8,128)(2,1)}, u32[]{:S(2)}, u32[]{:S(2)}) collective-permute-start(bf16[2,2,64,4096]{3,2,1,0:T(8,128)(2,1)} %constant_dynamic-update-slice_fusion.6.rest_2_), channel_id=1, source_target_pairs={{0,1},{1,0},{2,3},{3,2},{4,5},{5,4},{6,7},{7,6},{8,9},{9,8},{10,11... | collective-permute-start | bytes 6291464 | tf_op jit(solution)/shard_map/ppermute | solution.py:87
  151.7 46.3 %collective-permute-start.30 = (bf16[4,256,512]{2,1,0:T(8,128)(2,1)S(1)}, bf16[4,256,512]{2,1,0:T(8,128)(2,1)S(1)}, u32[]{:S(2)}, u32[]{:S(2)}) collective-permute-start(bf16[4,256,512]{2,1,0:T(8,128)(2,1)S(1)} %collective-permute-done.24.refs_4_.refs_0_), channel_id=1, source_target_pairs={{0,2},{1,3},{2,4},{3,5},{4,6},{5,7},{8,10},{9,11},{10,12},{11,13},... | collective-permute-start | bytes 3145736 | tf_op jit(solution)/shard_map/ppermute | solution.py:87
  302.7 40.1 %collective-permute-start.38 = (bf16[4,256,512]{2,1,0:T(8,128)(2,1)}, bf16[4,256,512]{2,1,0:T(8,128)(2,1)}, u32[]{:S(2)}, u32[]{:S(2)}) collective-permute-start(bf16[4,256,512]{2,1,0:T(8,128)(2,1)} %get-tuple-element.226), channel_id=1, source_target_pairs={{0,1},{1,0},{2,3},{3,2},{4,5},{5,4},{6,7},{7,6},{8,9},{9,8},{10,11... | collective-permute-start | bytes 3145736 | tf_op jit(solution)/shard_map/ppermute | solution.py:87
  305.8 36.9 %collective-permute-start.39 = (bf16[4,256,512]{2,1,0:T(8,128)(2,1)}, bf16[4,256,512]{2,1,0:T(8,128)(2,1)}, u32[]{:S(2)}, u32[]{:S(2)}) collective-permute-start(bf16[4,256,512]{2,1,0:T(8,128)(2,1)} %fusion.6), channel_id=1, source_target_pairs={{2,0},{3,1},{4,2},{5,3},{6,4},{7,5},{10,8},{11,9},{12,10},{13,11},... | collective-permute-start | bytes 3145736 | tf_op jit(solution)/shard_map/ppermute | solution.py:87
  312.8 40.8 %collective-permute-start.41 = (bf16[2,2,64,3072]{3,2,1,0:T(8,128)(2,1)}, bf16[2,2,64,3072]{3,2,1,0:T(8,128)(2,1)S(1)}, u32[]{:S(2)}, u32[]{:S(2)}) collective-permute-start(bf16[2,2,64,3072]{3,2,1,0:T(8,128)(2,1)} %fusion.7), channel_id=1, source_target_pairs={{0,16},{1,17},{2,18},{3,19},{4,20},{5,21},{6,22},{7,23},{8,24},{9,... | collective-permute-start | bytes 4718600 | tf_op jit(solution)/shard_map/ppermute | solution.py:87
  315.8 50.9 %collective-permute-start.42 = (bf16[2,2,64,3072]{3,2,1,0:T(8,128)(2,1)}, bf16[2,2,64,3072]{3,2,1,0:T(8,128)(2,1)}, u32[]{:S(2)}, u32[]{:S(2)}) collective-permute-start(bf16[2,2,64,3072]{3,2,1,0:T(8,128)(2,1)} %add_convert_fusion), channel_id=1, source_target_pairs={{0,8},{1,9},{2,10},{3,11},{4,12},{5,13},{6,14},{7,15},{8,0},{9,1},... | collective-permute-start | bytes 4718600 | tf_op jit(solution)/shard_map/ppermute | solution.py:87
  345.3 49.1 %collective-permute-start.40 = (bf16[4,256,512]{2,1,0:T(8,128)(2,1)S(1)}, bf16[4,256,512]{2,1,0:T(8,128)(2,1)S(1)}, u32[]{:S(2)}, u32[]{:S(2)}) collective-permute-start(bf16[4,256,512]{2,1,0:T(8,128)(2,1)S(1)} %fusion.1), channel_id=1, source_target_pairs={{2,0},{3,1},{4,2},{5,3},{6,4},{7,5},{10,8},{11,9},{12,10},{13,11},... | collective-permute-start | bytes 3145736 | tf_op jit(solution)/shard_map/ppermute | solution.py:87
  347.8 47.8 %collective-permute-start.37 = (bf16[4,256,512]{2,1,0:T(8,128)(2,1)}, bf16[4,256,512]{2,1,0:T(8,128)(2,1)}, u32[]{:S(2)}, u32[]{:S(2)}) collective-permute-start(bf16[4,256,512]{2,1,0:T(8,128)(2,1)} %get-tuple-element.159), channel_id=1, source_target_pairs={{0,1},{1,0},{2,3},{3,2},{4,5},{5,4},{6,7},{7,6},{8,9},{9,8},{10,11... | collective-permute-start | bytes 3145736 | tf_op jit(solution)/shard_map/ppermute | solution.py:87
  353.6 76.8 %collective-permute-start.36 = (bf16[4,256,512]{2,1,0:T(8,128)(2,1)S(1)}, bf16[4,256,512]{2,1,0:T(8,128)(2,1)}, u32[]{:S(2)}, u32[]{:S(2)}) collective-permute-start(bf16[4,256,512]{2,1,0:T(8,128)(2,1)S(1)} %get-tuple-element.158), channel_id=1, source_target_pairs={{0,1},{1,0},{2,3},{3,2},{4,5},{5,4},{6,7},{7,6},{8,9},{9,8},{10,11... | collective-permute-start | bytes 3145736 | tf_op jit(solution)/shard_map/ppermute | solution.py:87
  356.8 44.4 %collective-permute-start.44 = (bf16[1,2,64,3072]{3,2,1,0:T(8,128)(2,1)}, bf16[1,2,64,3072]{3,2,1,0:T(8,128)(2,1)}, u32[]{:S(2)}, u32[]{:S(2)}) collective-permute-start(bf16[1,2,64,3072]{3,2,1,0:T(8,128)(2,1)} %fusion.8), channel_id=1, source_target_pairs={{0,8},{1,9},{2,10},{3,11},{4,12},{5,13},{6,14},{7,15},{8,0},{9,1},... | collective-permute-start | bytes 2359304 | tf_op jit(solution)/shard_map/ppermute | solution.py:87
  369.0 32.1 %collective-permute-start.45 = (bf16[1,2,64,3072]{3,2,1,0:T(8,128)(2,1)}, bf16[1,2,64,3072]{3,2,1,0:T(8,128)(2,1)}, u32[]{:S(2)}, u32[]{:S(2)}) collective-permute-start(bf16[1,2,64,3072]{3,2,1,0:T(8,128)(2,1)} %add_convert_fusion.4), channel_id=1, source_target_pairs={{0,16},{1,17},{2,18},{3,19},{4,20},{5,21},{6,22},{7,23},{8,24},{9,... | collective-permute-start | bytes 2359304 | tf_op jit(solution)/shard_map/ppermute | solution.py:87
  394.4 71.3 %collective-permute-start.47 = (bf16[2,4,2,64,2048]{4,3,2,1,0:T(8,128)(2,1)}, bf16[2,4,2,64,2048]{4,3,2,1,0:T(8,128)(2,1)}, u32[]{:S(2)}, u32[]{:S(2)}) collective-permute-start(bf16[2,4,2,64,2048]{4,3,2,1,0:T(8,128)(2,1)} %get-tuple-element.171), channel_id=1, source_target_pairs={{0,1},{1,0},{2,3},{3,2},{4,5},{5,4},{6,7},{7,6},{8,9},{9,8},{10,11... | collective-permute-start | bytes 12582920 | tf_op jit(solution)/shard_map/ppermute | solution.py:87
  398.6 31.8 %collective-permute-start.43 = (bf16[4,256,512]{2,1,0:T(8,128)(2,1)}, bf16[4,256,512]{2,1,0:T(8,128)(2,1)}, u32[]{:S(2)}, u32[]{:S(2)}) collective-permute-start(bf16[4,256,512]{2,1,0:T(8,128)(2,1)} %fusion.3), channel_id=1, source_target_pairs={{2,0},{3,1},{4,2},{5,3},{6,4},{7,5},{10,8},{11,9},{12,10},{13,11},... | collective-permute-start | bytes 3145736 | tf_op jit(solution)/shard_map/ppermute | solution.py:87
  405.4 60.1 %collective-permute-start.46 = (bf16[64,3072]{1,0:T(8,128)(2,1)S(1)}, bf16[64,3072]{1,0:T(8,128)(2,1)S(1)}, u32[]{:S(2)}, u32[]{:S(2)}) collective-permute-start(bf16[64,3072]{1,0:T(8,128)(2,1)S(1)} %fusion.41), channel_id=1, source_target_pairs={{0,2},{1,3},{2,4},{3,5},{4,6},{5,7},{6,0},{7,1},{8,10},{9,11},{10,... | collective-permute-start | bytes 1179656 | tf_op jit(solution)/shard_map/ppermute | solution.py:87
  470.4 28.5 %collective-permute-start.49 = (bf16[2,2,64,2048]{3,2,1,0:T(8,128)(2,1)}, bf16[2,2,64,2048]{3,2,1,0:T(8,128)(2,1)}, u32[]{:S(2)}, u32[]{:S(2)}) collective-permute-start(bf16[2,2,64,2048]{3,2,1,0:T(8,128)(2,1)} %fusion.9), channel_id=1, source_target_pairs={{0,16},{1,17},{2,18},{3,19},{4,20},{5,21},{6,22},{7,23},{8,24},{9,... | collective-permute-start | bytes 3145736 | tf_op jit(solution)/shard_map/ppermute | solution.py:87
  488.1 28.5 %collective-permute-start.56 = (bf16[2,4,2,64,512]{4,3,2,1,0:T(8,128)(2,1)}, bf16[2,4,2,64,512]{4,3,2,1,0:T(8,128)(2,1)S(1)}, u32[]{:S(2)}, u32[]{:S(2)}) collective-permute-start(bf16[2,4,2,64,512]{4,3,2,1,0:T(8,128)(2,1)} %get-tuple-element.189), channel_id=1, source_target_pairs={{0,1},{1,0},{2,3},{3,2},{4,5},{5,4},{6,7},{7,6},{8,9},{9,8},{10,11... | collective-permute-start | bytes 3145736 | tf_op jit(solution)/shard_map/ppermute | solution.py:87
  525.6 27.2 %collective-permute-start.64 = (bf16[64,3072]{1,0:T(8,128)(2,1)S(1)}, bf16[64,3072]{1,0:T(8,128)(2,1)S(1)}, u32[]{:S(2)}, u32[]{:S(2)}) collective-permute-start(bf16[64,3072]{1,0:T(8,128)(2,1)S(1)} %fusion.23), channel_id=1, source_target_pairs={{0,2},{1,3},{2,4},{3,5},{4,6},{5,7},{6,0},{7,1},{8,10},{9,11},{10,... | collective-permute-start | bytes 1179656 | tf_op jit(solution)/shard_map/ppermute | solution.py:87
  (88 other events, 974.7 us)
where the time goes:
time: 590 us; the launch traced here: 580 us
  Pallas kernels  219 us (37%)
  waiting for transfers between devices  192 us (33%)
  starting transfers between devices  79.2 us (13%)
  other arithmetic  65.3 us (11%)
  local copies, waits for them, and re-layouts  22 us (4%)
    ppermute x70, waiting for transfers between devices, move(): return lax.ppermute(value, both, pairs)  192 us
    ppermute x70, starting transfers between devices, move(): return lax.ppermute(value, both, pairs)  79.2 us
    pallas_call x1, Pallas kernels, feed(): pl.pallas_call(functools.partial(feed_kernel, grid, span, split), grid_sp...  50.7 us
    pallas_call x3, Pallas kernels, weight_grad(): pl.pallas_call(functools.partial(weight_kernel, grid, shard, span, len(pa...  45.1 us
    pallas_call x2, Pallas kernels, attend_back(): pl.pallas_call(functools.partial(attend_back_kernel, n, acc is not None,...  37.8 us
    pallas_call x2, Pallas kernels, attend(): pl.pallas_call(functools.partial(attend_kernel, n, acc is not None, finis...  24.9 us
    convert_element_type x12, other arithmetic, go(): value = sum((p[given].astype(f32) for p in parts)).astype(bf16)  23.5 us
    pallas_call x2, Pallas kernels, project(): pl.pallas_call(functools.partial(project_kernel, grid, normed // 128, hea...  22.6 us
  transfers between devices with their start and end apart: 70, of which 29 were waited for; matrix products, arithmetic and copies ran while one was open for 14% of the time, Pallas kernels for 25%

commit v1 on v0

--- a/solution.py
+++ b/solution.py
@@ -92,8 +92,8 @@
     def partner(self, value):
         return self.move(value, lambda r, s: (r, s ^ 1))
 
-    def around(self, value):
-        return self.move(value, lambda r, s: (r, (s + 2) % self.seqs))
+    def around(self, value, steps=1):
+        return self.move(value, lambda r, s: (r, (s + 2 * steps) % self.seqs))
 
     def up(self, value):
         return self.move(value, lambda r, s: (r, s + 2) if s + 2 < self.seqs else None)
@@ -133,19 +133,9 @@
                 held = [jnp.concatenate([held[k], found[k]], axis=0) for k in range(2)]
         return pieces, arrived
 
-    def with_partner(self, pieces, merge):
-        if merge:
-            pieces = [jnp.stack(pieces)]
-        return pieces + [self.partner(p) for p in pieces]
-
-    def everywhere(self, value):
-        for bit in self.orders[0]:
-            value = value + self.across(value, bit)
-        bit = 1
-        while bit < self.seqs:
-            value = value + self.move(value, lambda r, s, bit=bit: (r, s ^ bit))
-            bit *= 2
-        return value
+    def with_partner(self, pieces, *waits):
+        pieces = jnp.stack(pieces)
+        return [pieces, self.partner(after(pieces, *waits) if waits else pieces)]
 
 
 class Order:
@@ -167,9 +157,38 @@
         return after(value, self.kernel)
 
 
+class Everywhere:
+    def __init__(self, grid, order, value):
+        self.grid, self.order, self.total = grid, order, value
+        self.flight = []
+        self.moves = [(bit, 0) for bit in grid.orders[0]]
+        self.moves += [(0, 1 << k) for k in range(grid.seqs.bit_length() - 1)]
+
+    def land(self):
+        came, self.flight = [self.order.late(c) for c in self.flight], []
+        for each in came:
+            self.total = self.total + each
+        return came
+
+    def go(self):
+        self.land()
+        if not self.moves:
+            return []
+        row, seq = self.moves.pop(0)
+        sent = self.order.late(self.total)
+        self.flight = [self.grid.move(sent, lambda r, s: (r ^ row, s ^ seq))]
+        return [sent]
+
+    def finish(self):
+        while self.go():
+            pass
+        return self.total
+
+
 class Sum:
-    def __init__(self, grid, order, parts):
+    def __init__(self, grid, order, parts, direct=False):
         mine, self.theirs = parts
+        self.direct = direct
         self.grid = grid
         self.order = order
         self.halves = [[mine[half]] for half in range(2)]
@@ -192,6 +211,8 @@
             elif self.stage <= 1 + self.row_stages:
                 for half in range(2):
                     self.halves[half].append(came[half])
+            elif self.direct:
+                self.total = self.total + sum(c.astype(f32) for c in came)
             else:
                 self.total = came[0].astype(f32) + self.at(self.stage - self.row_stages)
         return came
@@ -216,6 +237,17 @@
                 self.halves[half] = [p[kept] for p in parts]
                 sent.append(late(value))
                 self.flight.append(grid.across(sent[half], bit))
+        elif self.direct:
+            if self.total is not None:
+                return []
+            self.levels = jnp.concatenate(
+                [sum(p[0].astype(f32) for p in parts) for parts in self.halves], axis=0
+            )
+            self.total = self.at(0)
+            sent = [
+                late(self.at(grid.depth - step).astype(bf16)) for step in range(1, grid.depth)
+            ]
+            self.flight = [grid.around(each, k + 1) for k, each in enumerate(sent)]
         elif self.stage < self.row_stages + grid.depth:
             if self.total is None:
                 self.levels = jnp.concatenate(
@@ -526,7 +558,7 @@
     chunks, refs = refs[:n], refs[n:]
     if with_acc:
         acc_in, refs = refs[0], refs[1:]
-    grads_out, dq_ref, buffer, sems, acc, q_wide, do_wide = refs
+    own_ref, their_ref, dq_ref, buffer, sems, acc, q_wide, do_wide, grads_out = refs
     seq, n_seqs = pl.program_id(0), pl.num_programs(0)
     span = q_ref.shape[1]
     n_heads = q_ref.shape[2] // 256
@@ -584,8 +616,8 @@
                         return pltpu.roll(total, 64, 1) if parity else total
 
                     dtype = grads_out.dtype
-                    grads_out[chunk, 0, :, k_lanes] += joined(both_k).astype(dtype)
-                    grads_out[chunk, 0, :, v_lanes] += joined(both_v).astype(dtype)
+                    grads_out[chunk, :, k_lanes] += joined(both_k).astype(dtype)
+                    grads_out[chunk, :, v_lanes] += joined(both_v).astype(dtype)
 
                 @pl.when(whole)
                 def _():
@@ -602,6 +634,8 @@
 
     for head in range(n_heads):
         one_head(head)
+    own_ref[:, 0] = grads_out[: n // 2]
+    their_ref[:, 0] = grads_out[n // 2 :]
 
 
 def attend_back(info, bases, queries, grad_out, out, logs, chunks, acc=None, finish=True):
@@ -621,25 +655,25 @@
         dq_shape, dq_spec = jax.ShapeDtypeStruct(queries.shape, bf16), q_spec
     else:
         dq_shape, dq_spec = acc_shape, acc_spec
-    grads, dq = pl.pallas_call(
+    grad_shape = jax.ShapeDtypeStruct((n // 2, seqs, span, kv_width), bf16)
+    grad_spec = pl.BlockSpec((n // 2, 1, span, kv_width), lambda b, *_: (0, b, 0, 0))
+    return pl.pallas_call(
         functools.partial(attend_back_kernel, n, acc is not None, finish),
         grid_spec=pltpu.PrefetchScalarGridSpec(
             num_scalar_prefetch=1,
             grid=(seqs,),
             in_specs=in_specs,
-            out_specs=[
-                pl.BlockSpec((n, 1, span, kv_width), lambda b, *_: (0, b, 0, 0)),
-                dq_spec,
-            ],
+            out_specs=[grad_spec, grad_spec, dq_spec],
             scratch_shapes=[
                 pltpu.VMEM((2, n, span, kv_width), bf16),
                 pltpu.SemaphoreType.DMA((2, n)),
                 pltpu.VMEM((128, 2 * span), f32),
                 pltpu.VMEM((2 * span, 256), bf16),
                 pltpu.VMEM((2 * span, 256), bf16),
+                pltpu.VMEM((n, span, kv_width), bf16),
             ],
         ),
-        out_shape=[jax.ShapeDtypeStruct((n, seqs, span, kv_width), bf16), dq_shape],
+        out_shape=[grad_shape, grad_shape, dq_shape],
         compiler_params=params(1),
         cost_estimate=pl.CostEstimate(
             flops=10 * 4 * seqs * span * width * span * n,
@@ -647,7 +681,6 @@
             transcendentals=seqs * span * width // 64 * span * n,
         ),
     )(jnp.concatenate([info, bases]), *args)
-    return [grads[i] for i in range(n)] + [dq]
 
 
 def unproject_kernel(
@@ -736,18 +769,13 @@
     out_ref, hidden_ref, mid_ref, dgu_ref, dmid_ref, dheads_ref, *rest = rest
     w_out, w_gu, w_down, out_sems, gu_sems, down_sems = rest
     a, b = split
+    out_loads = lambda: loads(grid, place_ref, pieces, w_out, out_sems, (0, a))
+    gu_loads = lambda: loads(grid, place_ref, pieces, w_gu, gu_sems, (2 * a, 2 * a + b))
+    down_loads = lambda: loads(grid, place_ref, pieces, w_down, down_sems, (a, 2 * a))
 
     @pl.when(pl.program_id(0) == 0)
     def _():
-        copies = (
-            loads(grid, place_ref, pieces, w_out, out_sems, (0, a))
-            + loads(grid, place_ref, pieces, w_gu, gu_sems, (2 * a, 2 * a + b))
-            + loads(grid, place_ref, pieces, w_down, down_sems, (a, 2 * a))
-        )
-        for copy in copies:
-            copy.start()
-        for copy in copies:
-            copy.wait()
+        load_all(out_loads() + gu_loads() + down_loads())
 
     rows = tok_ref.shape[0]
     middle = tok_ref[...].astype(f32) + mm(heads_ref[...], w_out[...], NT)
@@ -1038,24 +1066,28 @@
 
     order = Order()
     depth = grid.depth
+    split = max(1, depth // 2)
     kv_steps = grid.ring(qkv_shard[:, query_width:])
     kv_own, kv_came = grid.spread(kv_steps)
-    q_steps = grid.ring(
-        qkv_shard[:, :query_width], [[], [kv_steps[2]]] + [[kv_steps[-1]]] * (depth - 3)
-    )
+    q_steps = grid.ring(qkv_shard[:, :query_width], [[kv_steps[1]], [kv_steps[-1]]])[:3]
     feed_steps = grid.ring(
-        jnp.concatenate([w_out, w_down, gateup_shard], axis=1),
-        [[kv_steps[1]], kv_came[0]] + [kv_came[-1]] * (depth - 3),
-    )
-    kv_pieces = grid.with_partner(kv_own, True)
-    q_own, q_came = grid.spread(q_steps, [kv_came[-1]])
-    q_pieces = grid.with_partner(q_own, True)
-    feed_own, feed_came = grid.spread(feed_steps, [q_came[-1]])
+        jnp.concatenate([w_out, w_down, gateup_shard], axis=1), [[kv_steps[2]], kv_came[-1]]
+    )[:3]
+    kv_pieces = grid.with_partner(kv_own, feed_steps[1], q_steps[1])
 
     rows_in = tokens.reshape(row_count, model_width)
     kv, k_raw, scale1 = project(grid, rows_in, kv_pieces, k_gain_f, tables, kv_width, head_dim)
     order.leave(kv)
+    while len(feed_steps) < depth:
+        feed_steps.append(grid.around(after(feed_steps[-1], kv)))
+        q_steps.append(grid.around(after(q_steps[-1], kv)))
+    q_own, q_came = grid.spread(q_steps, [[kv]] + [feed_steps[2:3]] * (len(grid.orders[0]) - 1))
+    feed_own, feed_came = grid.spread(feed_steps, [q_came[-1]])
     kv = kv.reshape(seq_count, span_len, 2 * kv_width)
+    reach = [kv]
+    for _ in range(1, depth - 1):
+        reach.append(grid.up(reach[-1]))
+    q_pieces = grid.with_partner(q_own, reach[1], feed_steps[-1])
     q, q_raw = project(
         grid,
         order.enter(rows_in),
@@ -1067,31 +1099,30 @@
         scale1,
     )
     order.leave(q)
-    order.pin(*feed_came[0])
-    feed_held = [grid.partner(order.late(feed_own[k])) for k in (0, 2)]
     q = q.reshape(seq_count, span_len, query_width)
-
-    reach = [kv]
-    for step in range(1, depth):
-        held = reach[-1] if step == 1 else order.late(reach[-1])
-        reach.append(grid.up(held))
-    chunks, bases = [], []
+    bases = []
     for step in range(depth):
         level = grid.level - step
         start = jnp.stack([level * 2 + grid.core, level * 2 + 1 - grid.core]) * span_len
         bases.append(jnp.where(level >= 0, start, -1).astype(jnp.int32))
-    chunks = [(own, grid.partner(own)) for own in reach[:-1]]
-    near = [c for pair in chunks for c in pair]
+    reach[-1] = order.late(reach[-1])
+    reach.append(grid.up(reach[-1]))
+    crossed = [grid.partner(own) for own in reach[:-1]]
+    order.pin(*feed_came[0])
+    feed_held = [grid.partner(order.late(feed_own[k])) for k in (0, 2)]
+    near = [c for pair in zip(reach[:-1], crossed) for c in pair]
     acc = attend(info, jnp.concatenate(bases[:-1]), order.enter(q), near, None, False)
     order.leave(acc)
+    order.pin(*feed_came[-1], *feed_held)
     feed_found = [grid.partner(order.late(feed_own[k])) for k in (1, 3)]
-    order.pin(*feed_came[-1], *feed_held)
-    feed_pieces = feed_own + [feed_held[0], feed_found[0], feed_held[1], feed_found[1]]
-    farthest = order.late(reach[-1])
-    chunks.append((farthest, grid.partner(farthest)))
-    heads, logs = attend(info, bases[-1], order.enter(q), list(chunks[-1]), acc, True)
+    reach[-1] = order.late(reach[-1])
+    crossed.append(grid.partner(reach[-1]))
+    heads, logs = attend(
+        info, bases[-1], order.enter(q), [reach[-1], crossed[-1]], acc, True
+    )
     order.leave(heads)
     attended = heads.reshape(row_count, query_width)
+    feed_pieces = feed_own + [feed_held[0], feed_found[0], feed_held[1], feed_found[1]]
 
     flat_cot = cotangent.reshape(row_count, model_width)
     output, hidden, middle, grad_gu, grad_mid, grad_heads = feed(
@@ -1114,60 +1145,44 @@
 
     kv_flight = []
 
-    def kv_hop(own, other):
+    def kv_sum_here(own, other):
         kv_flight[:] = [order.late(came) for came in kv_flight]
-        order.pin(other, *kv_flight)
         here = own.astype(f32) + other.astype(f32)
         for came in kv_flight:
             here = here + came.astype(f32)
-        sent = order.late(here.astype(bf16))
+        return here.astype(bf16)
+
+    def kv_hop(own, other):
+        sent = order.late(kv_sum_here(own, other))
         order.pin(sent)
         kv_flight[:] = [grid.down(sent)]
+
+    def back(steps, acc, final):
+        chosen = [reach[k] for k in steps] + [crossed[k] for k in steps]
+        starts = jnp.stack([bases[k] for k in steps], axis=1).reshape(-1)
+        return attend_back(
+            info, starts, order.enter(q), grad_heads, heads, logs, chosen, acc, final
+        )
 
     feed_sum = Sum(
         grid,
         order,
-        weight_grad(grid, info, span_len, (flat_cot, hidden), (middle, grad_gu)),
+        weight_grad(
+            grid, info, span_len, (flat_cot, order.enter(hidden)), (middle, grad_gu)
+        ),
     )
     order.leave(feed_sum.theirs)
     advance(feed_sum)
-
-    split = max(1, depth // 2)
-    far = [c for pair in chunks[split:] for c in pair]
-    near = [c for pair in chunks[:split] for c in pair]
-    *far_grads, acc_q = attend_back(
-        info,
-        jnp.concatenate(bases[split:]),
-        order.enter(q),
-        grad_heads,
-        heads,
-        logs,
-        far,
-        None,
-        False,
-    )
+    far_own, far_theirs, acc_q = back(range(split, depth), None, False)
     order.leave(acc_q)
-    far_grads = [far_grads[2 * k : 2 * k + 2] for k in range(depth - split)]
-    crossed = [grid.partner(other) for _, other in far_grads]
-    kv_hop(far_grads[-1][0], crossed[-1])
+    far_came = grid.partner(far_theirs)
+    kv_hop(far_own[-1], far_came[-1])
     advance(feed_sum)
-    *near_grads, grad_q = attend_back(
-        info,
-        jnp.concatenate(bases[:split]),
-        order.enter(q),
-        grad_heads,
-        heads,
-        logs,
-        near,
-        acc_q,
-        True,
-    )
+    near_own, near_theirs, grad_q = back(range(split), acc_q, True)
     order.leave(grad_q)
-    near_grads = [near_grads[2 * k : 2 * k + 2] for k in range(split)]
-    crossed = [grid.partner(order.late(other)) for _, other in near_grads] + crossed
-    all_grads = near_grads + far_grads
+    near_came = grid.partner(order.late(near_theirs))
     for step in reversed(range(split, depth - 1)):
-        kv_hop(all_grads[step][0], crossed[step])
+        kv_hop(far_own[step - split], far_came[step - split])
     advance(feed_sum)
     grad_pq, gq = unproject(
         info,
@@ -1188,27 +1203,19 @@
     )
     order.leave(square_sum.theirs)
     for step in reversed(range(1, split)):
-        kv_hop(all_grads[step][0], crossed[step])
+        kv_hop(near_own[step], near_came[step])
     advance(feed_sum, square_sum)
     back_q = query_back(grid, info, order.enter(grad_pq), q_pieces, model_width, span_len)
     order.leave(back_q)
-
-    kv_flight = [order.late(came) for came in kv_flight]
-    order.pin(*kv_flight)
     advance(feed_sum, square_sum)
-    grad_kv = all_grads[0][0].astype(f32) + crossed[0].astype(f32)
-    for came in kv_flight:
-        grad_kv = grad_kv + came.astype(f32)
-    grad_kv = grad_kv.astype(bf16).reshape(row_count, 2 * kv_width)
+    grad_kv = kv_sum_here(near_own[0], near_came[0]).reshape(row_count, 2 * kv_width)
     grad_pkv, gk = unproject(
         info, order.enter(grad_kv), k_raw, scale1, k_gain_f, tables, head_dim
     )
-    order.leave(grad_pkv)
-    kv_sum = Sum(
-        grid, order, weight_grad(grid, info, span_len, (rows_in, order.enter(grad_pkv)))
-    )
+    kv_sum = Sum(grid, order, weight_grad(grid, info, span_len, (rows_in, grad_pkv)), True)
     order.leave(kv_sum.theirs)
-    advance(feed_sum, square_sum, kv_sum)
+    gain_sum = Everywhere(grid, order, jnp.concatenate([gq[:1], gk[:1]], axis=0))
+    advance(feed_sum, square_sum, kv_sum, gain_sum)
     grad_tokens = last(
         grid,
         info,
@@ -1221,7 +1228,7 @@
         span_len,
     )
     order.leave(grad_tokens)
-    gains = grid.everywhere(jnp.concatenate([gq[:1], gk[:1]], axis=0))
+    gains = gain_sum.finish()
     gains = gains[:, :head_dim] + gains[:, head_dim:]
     kv_total, square_total, feed_total = kv_sum.finish(), square_sum.finish(), feed_sum.finish()
     sum_qkv = jnp.concatenate([square_total[:, :query_width], kv_total], axis=1)

time: 590 us -> 569 us (0.964)
  waiting for transfers between devices: 192 us -> 181 us
  other arithmetic: 65.3 us -> 55.2 us
    ppermute x70 -> x68, waiting for transfers between devices: 192 us -> 181 us  [move(): return lax.ppermute(value, both, pairs)]
    ppermute x70 -> x68, starting transfers between devices: 79.2 us -> 79.8 us  [move(): return lax.ppermute(value, both, pairs)]
  transfers between devices with their start and end apart: 70 -> 68, of which waited for: 29 -> 26; matrix products, arithmetic and copies ran while one was open for 14% -> 12% of each run, Pallas kernels for 25% -> 26%
where the time goes in v1:
time: 569 us; the launch traced here: 559 us
  Pallas kernels  219 us (38%)
  waiting for transfers between devices  181 us (32%)
  starting transfers between devices  79.8 us (14%)
  other arithmetic  55.2 us (10%)
  local copies, waits for them, and re-layouts  21.6 us (4%)
    ppermute x68, waiting for transfers between devices, move(): return lax.ppermute(value, both, pairs)  181 us
    ppermute x68, starting transfers between devices, move(): return lax.ppermute(value, both, pairs)  79.8 us
    pallas_call x1, Pallas kernels, feed(): pl.pallas_call(functools.partial(feed_kernel, grid, span, split), grid_sp...  50.7 us
    pallas_call x3, Pallas kernels, weight_grad(): pl.pallas_call(functools.partial(weight_kernel, grid, shard, span, len(pa...  45.2 us
    pallas_call x2, Pallas kernels, attend_back(): pl.pallas_call(functools.partial(attend_back_kernel, n, acc is not None,...  38 us
    pallas_call x2, Pallas kernels, attend(): pl.pallas_call(functools.partial(attend_kernel, n, acc is not None, finis...  24.9 us
    pallas_call x2, Pallas kernels, project(): pl.pallas_call(functools.partial(project_kernel, grid, normed // 128, hea...  22.4 us
    convert_element_type x12, other arithmetic, go(): value = sum((p[given].astype(f32) for p in parts)).astype(bf16)  19.6 us
  transfers between devices with their start and end apart: 68, of which 26 were waited for; matrix products, arithmetic and copies ran while one was open for 12% of the time, Pallas kernels for 26%

profile of v1, /device:TPU:0, one launch (start us, length us, event | category | flops | bytes accessed | tf_op | source)
XLA Modules:
  0.0 558.9 jit_solution(4542946696623173105)
XLA Ops:
  44.4 9.3 %shard_map.186 = (bf16[1024,512]{1,0:T(8,128)(2,1)}, bf16[1024,256]{1,0:T(8,128)(2,1)}, f32[1024,128]{1,0:T(8,128)}) custom-call(s32[3]{0:T(128)} %pad_add_fusion.3.place_ref, bf16[1024,2048]{1,0:T(8,128)(2,1)} %bitcast.201, bf16[4,2,2,64,512]{4,3,2,1,0:T(8,128)(2,1)} %copy-done.2, bf16[4,2,2,64,512]{4,3,2,1,0:T(8,128)(2,1)} %copy-done.8, ...), custom_call_target="tpu_custom_call" | custom-call | flops 4294967296 | bytes 8388608 | tf_op jit(solution)/shard_map/pallas_call | solution.py:359
  56.1 9.1 %collective-permute-done.14 = bf16[64,1024]{1,0:T(8,128)(2,1)S(1)} collective-permute-done((bf16[64,1024]{1,0:T(8,128)(2,1)S(1)}, bf16[64,1024]{1,0:T(8,128)(2,1)S(1)}, u32[]{:S(2)}, u32[]{:S(2)}) %collective-permute-start.14) | collective-permute-done | bytes 131104 | tf_op jit(solution)/shard_map/ppermute | solution.py:87
  76.1 8.3 %collective-permute-done.12 = bf16[2,2,64,1024]{3,2,1,0:T(8,128)(2,1)S(1)} collective-permute-done((bf16[2,2,64,1024]{3,2,1,0:T(8,128)(2,1)S(1)}, bf16[2,2,64,1024]{3,2,1,0:T(8,128)(2,1)S(1)}, u32[]{:S(2)}, u32[]{:S(2)}) %collective-permute-start.12) | collective-permute-done | bytes 524320 | tf_op jit(solution)/shard_map/ppermute | solution.py:87
  86.3 14.5 %collective-permute-done.18 = bf16[64,4096]{1,0:T(8,128)(2,1)S(1)} collective-permute-done((bf16[64,4096]{1,0:T(8,128)(2,1)S(1)}, bf16[64,4096]{1,0:T(8,128)(2,1)S(1)}, u32[]{:S(2)}, u32[]{:S(2)}) %collective-permute-start.18) | collective-permute-done | bytes 524320 | tf_op jit(solution)/shard_map/ppermute | solution.py:87
  113.8 13.1 %shard_map.187 = (bf16[1024,1024]{1,0:T(8,128)(2,1)}, bf16[1024,1024]{1,0:T(8,128)(2,1)}) custom-call(s32[3]{0:T(128)} %pad_add_fusion.3.place_ref, bf16[1024,2048]{1,0:T(8,128)(2,1)} %bitcast.202, bf16[4,2,2,64,1024]{4,3,2,1,0:T(8,128)(2,1)} %copy-done.3, bf16[4,2,2,64,1024]{4,3,2,1,0:T(8,128)(2,1)} %collective-permute-done.19.rest_1_, ...), custom_call_target="tpu_custom_call" | custom-call | flops 8589934592 | bytes 12582912 | tf_op jit(solution)/shard_map/pallas_call | solution.py:359
  126.9 7.2 %collective-permute-done.24.refs_4_.refs_0_ = bf16[4,256,512]{2,1,0:T(8,128)(2,1)} collective-permute-done((bf16[4,256,512]{2,1,0:T(8,128)(2,1)}, bf16[4,256,512]{2,1,0:T(8,128)(2,1)}, u32[]{:S(2)}, u32[]{:S(2)}) %collective-permute-start.24) | collective-permute-done | bytes 1048608 | tf_op jit(solution)/shard_map/ppermute | solution.py:87
  143.7 16.9 %shard_map.188.refs_2_ = f32[4,4,512,256]{3,2,1,0:T(8,128)} custom-call(s32[11]{0:T(128)} %concatenate.123.info_ref, bf16[4,256,1024]{2,1,0:T(8,128)(2,1)} %bitcast.227, bf16[4,256,512]{2,1,0:T(8,128)(2,1)} %bitcast.28.refs_0_, bf16[4,256,512]{2,1,0:T(8,128)(2,1)} %collective-permute-done.22.refs_1_.refs_2_, ...), custom_call_target="tpu_custom_call" | custom-call | flops 25769803776 | bytes 25165824 | tf_op jit(solution)/shard_map/pallas_call | solution.py:534
  160.5 24.4 %collective-permute-done.27.rest_3_ = bf16[2,2,64,4096]{3,2,1,0:T(8,128)(2,1)} collective-permute-done((bf16[2,2,64,4096]{3,2,1,0:T(8,128)(2,1)S(1)}, bf16[2,2,64,4096]{3,2,1,0:T(8,128)(2,1)}, u32[]{:S(2)}, u32[]{:S(2)}) %collective-permute-start.27) | collective-permute-done | bytes 2097184 | tf_op jit(solution)/shard_map/ppermute | solution.py:87
  187.7 6.2 %collective-permute-done.31.refs_1_.refs_3_ = bf16[4,256,512]{2,1,0:T(8,128)(2,1)} collective-permute-done((bf16[4,256,512]{2,1,0:T(8,128)(2,1)}, bf16[4,256,512]{2,1,0:T(8,128)(2,1)}, u32[]{:S(2)}, u32[]{:S(2)}) %collective-permute-start.31) | collective-permute-done | bytes 1048608 | tf_op jit(solution)/shard_map/ppermute | solution.py:87
  193.9 8.0 %shard_map.189 = (bf16[4,256,1024]{2,1,0:T(8,128)(2,1)}, bf16[4,256,1024]{2,1,0:T(8,128)(2,1)}) custom-call(s32[7]{0:T(128)} %pad_add_fusion.4.info_ref, bf16[4,256,1024]{2,1,0:T(8,128)(2,1)} %bitcast.228, bf16[4,256,512]{2,1,0:T(8,128)(2,1)} %collective-permute-done.30.refs_0_.refs_1_, bf16[4,256,512]{2,1,0:T(8,128)(2,1)} %collective-permute-done.31.refs_1_.refs_3_, ...), custom_call_target="tpu_custom_call" | custom-call | flops 8589934592 | bytes 16777216 | tf_op jit(solution)/shard_map/pallas_call | solution.py:534
  201.9 50.7 %shard_map.190 = (bf16[1024,2048]{1,0:T(8,128)(2,1)}, bf16[1024,1024]{1,0:T(8,128)(2,1)}, bf16[1024,2048]{1,0:T(8,128)(2,1)}, bf16[1024,2048]{1,0:T(8,128)(2,1)}...) custom-call(s32[5]{0:T(128)} %pad_add_fusion.2.info_ref, s32[3]{0:T(128)} %pad_add_fusion.3.place_ref, ...), custom_call_target="tpu_custom_call" | custom-call | flops 51539607552 | bytes 48234496 | tf_op jit(solution)/shard_map/pallas_call | solution.py:836
  252.7 22.1 %shard_map.191 = (bf16[2,4,2,64,3072]{4,3,2,1,0:T(8,128)(2,1)}, bf16[2,4,2,64,3072]{4,3,2,1,0:T(8,128)(2,1)}) custom-call(s32[3]{0:T(128)} %pad_add_fusion.3.place_ref, s32[5]{0:T(128)} %pad_add_fusion.2.info_ref, bf16[1024,2048]{1,0:T(8,128)(2,1)} %bitcast.225, bf16[1024,2048]{1,0:T(8,128)(2,1)} %get-tuple-element.159.refs_1_, ...), custom_call_target="tpu_custom_call" | custom-call | flops 12884901888 | bytes 27262976 | tf_op jit(solution)/shard_map/pallas_call | solution.py:1002
  274.8 11.1 %shard_map.192 = (bf16[2,4,256,512]{3,2,1,0:T(8,128)(2,1)}, bf16[2,4,256,512]{3,2,1,0:T(8,128)(2,1)}, f32[4,4,128,512]{3,2,1,0:T(8,128)}) custom-call(s32[9]{0:T(128)} %get-tuple-element.281.info_ref, bf16[4,256,1024]{2,1,0:T(8,128)(2,1)} %bitcast.229, bf16[4,256,1024]{2,1,0:T(8,128)(2,1)} %bitcast.233, bf16[4,256,1024]{2,1,0:T(8,128)(2,1)} %get-tuple-element.155.o_ref, ...), custom_call_target="tpu_custom_call" | custom-call | flops 42949672960 | bytes 33554432 | tf_op jit(solution)/shard_map/pallas_call | solution.py:660
  302.8 26.8 %shard_map.193 = (bf16[2,4,256,512]{3,2,1,0:T(8,128)(2,1)}, bf16[2,4,256,512]{3,2,1,0:T(8,128)(2,1)}, bf16[4,256,1024]{2,1,0:T(8,128)(2,1)}) custom-call(s32[9]{0:T(128)} %get-tuple-element.280.info_ref, bf16[4,256,1024]{2,1,0:T(8,128)(2,1)} %bitcast.230, bf16[4,256,1024]{2,1,0:T(8,128)(2,1)} %bitcast.234, bf16[4,256,1024]{2,1,0:T(8,128)(2,1)} %get-tuple-element.155.o_ref, ...), custom_call_target="tpu_custom_call" | custom-call | flops 42949672960 | bytes 33554432 | tf_op jit(solution)/shard_map/pallas_call | solution.py:660
  348.9 8.6 %shard_map.194 = (bf16[1024,1024]{1,0:T(8,128)(2,1)}, f32[8,128]{1,0:T(8,128)}) custom-call(s32[5]{0:T(128)} %pad_add_fusion.2.info_ref, bf16[1024,1024]{1,0:T(8,128)(2,1)} %bitcast.208, bf16[1024,1024]{1,0:T(8,128)(2,1)} %get-tuple-element.187.raw_ref, f32[1024,128]{1,0:T(8,128)} %get-tuple-element.145.rest_6_.scale_ref, ...), custom_call_target="tpu_custom_call" | custom-call | flops 1073741824 | bytes 6291456 | tf_op jit(solution)/shard_map/pallas_call | solution.py:735
  358.2 16.1 %shard_map.195 = (bf16[2,4,2,64,2048]{4,3,2,1,0:T(8,128)(2,1)}, bf16[2,4,2,64,2048]{4,3,2,1,0:T(8,128)(2,1)}) custom-call(s32[3]{0:T(128)} %pad_add_fusion.3.place_ref, s32[5]{0:T(128)} %pad_add_fusion.2.info_ref, bf16[1024,2048]{1,0:T(8,128)(2,1)} %bitcast.204, bf16[1024,2048]{1,0:T(8,128)(2,1)} %get-tuple-element.181.refs_1_.dmid_ref, ...), custom_call_target="tpu_custom_call" | custom-call | flops 8589934592 | bytes 20971520 | tf_op jit(solution)/shard_map/pallas_call | solution.py:1002
  386.7 7.9 %collective-permute-start.44 = (bf16[64,3072]{1,0:T(8,128)(2,1)S(1)}, bf16[64,3072]{1,0:T(8,128)(2,1)S(1)}, u32[]{:S(2)}, u32[]{:S(2)}) collective-permute-start(bf16[64,3072]{1,0:T(8,128)(2,1)S(1)} %fusion.38), channel_id=1, source_target_pairs={{0,2},{1,3},{2,4},{3,5},{4,6},{5,7},{6,0},{7,1},{8,10},{9,11},{10,... | collective-permute-start | bytes 1179656 | tf_op jit(solution)/shard_map/ppermute | solution.py:87
  394.7 10.9 %shard_map.196.back_ref = f32[1024,2048]{1,0:T(8,128)} custom-call(s32[5]{0:T(128)} %pad_add_fusion.2.info_ref, s32[3]{0:T(128)} %pad_add_fusion.3.place_ref, bf16[1024,1024]{1,0:T(8,128)(2,1)} %get-tuple-element.196.refs_2_.grad_ref, bf16[4,2,2,64,1024]{4,3,2,1,0:T(8,128)(2,1)} %copy-done.3, bf16[4,2,2,64,1024]{4,3,2,1,0:T(8,128)(2,1)} %collective-permute-done.19.rest_1_), custom_call_target="tpu_custom_call" | custom-call | flops 4294967296 | bytes 14680064 | tf_op jit(solution)/shard_map/pallas_call | solution.py:883
  405.6 40.5 %collective-permute-done.44 = bf16[64,3072]{1,0:T(8,128)(2,1)S(1)} collective-permute-done((bf16[64,3072]{1,0:T(8,128)(2,1)S(1)}, bf16[64,3072]{1,0:T(8,128)(2,1)S(1)}, u32[]{:S(2)}, u32[]{:S(2)}) %collective-permute-start.44) | collective-permute-done | bytes 393248 | tf_op jit(solution)/shard_map/ppermute | solution.py:87
  465.8 7.0 %shard_map.198 = (bf16[2,4,2,64,512]{4,3,2,1,0:T(8,128)(2,1)}, bf16[2,4,2,64,512]{4,3,2,1,0:T(8,128)(2,1)}) custom-call(s32[3]{0:T(128)} %pad_add_fusion.3.place_ref, s32[5]{0:T(128)} %pad_add_fusion.2.info_ref, bf16[1024,2048]{1,0:T(8,128)(2,1)} %bitcast.205, bf16[1024,512]{1,0:T(8,128)(2,1)} %get-tuple-element.217.refs_1_.grad_ref), custom_call_target="tpu_custom_call" | custom-call | flops 2147483648 | bytes 7340032 | tf_op jit(solution)/shard_map/pallas_call | solution.py:1002
  474.5 6.6 %collective-permute-done.47 = bf16[2,2,64,2048]{3,2,1,0:T(8,128)(2,1)} collective-permute-done((bf16[2,2,64,2048]{3,2,1,0:T(8,128)(2,1)}, bf16[2,2,64,2048]{3,2,1,0:T(8,128)(2,1)}, u32[]{:S(2)}, u32[]{:S(2)}) %collective-permute-start.47) | collective-permute-done | bytes 1048608 | tf_op jit(solution)/shard_map/ppermute | solution.py:87
  487.4 13.1 %shard_map.199 = bf16[1024,2048]{1,0:T(8,128)(2,1)} custom-call(s32[5]{0:T(128)} %pad_add_fusion.2.info_ref, s32[3]{0:T(128)} %pad_add_fusion.3.place_ref, bf16[1024,2048]{1,0:T(8,128)(2,1)} %bitcast.206, bf16[1024,512]{1,0:T(8,128)(2,1)} %get-tuple-element.217.refs_1_.grad_ref, f32[1024,2048]{1,0:T(8,128)} %shard_map.196.back_ref, ...), custom_call_target="tpu_custom_call" | custom-call | flops 2147483648 | bytes 24117248 | tf_op jit(solution)/shard_map/pallas_call | solution.py:932
  519.4 9.0 %collective-permute-done.49 = bf16[1,2,64,2048]{3,2,1,0:T(8,128)(2,1)S(1)} collective-permute-done((bf16[1,2,64,2048]{3,2,1,0:T(8,128)(2,1)S(1)}, bf16[1,2,64,2048]{3,2,1,0:T(8,128)(2,1)S(1)}, u32[]{:S(2)}, u32[]{:S(2)}) %collective-permute-start.49) | collective-permute-done | bytes 524320 | tf_op jit(solution)/shard_map/ppermute | solution.py:87
  532.2 6.5 %collective-permute-done.51 = bf16[64,2048]{1,0:T(8,128)(2,1)S(1)} collective-permute-done((bf16[64,2048]{1,0:T(8,128)(2,1)S(1)}, bf16[64,2048]{1,0:T(8,128)(2,1)S(1)}, u32[]{:S(2)}, u32[]{:S(2)}) %collective-permute-start.51) | collective-permute-done | bytes 262176 | tf_op jit(solution)/shard_map/ppermute | solution.py:87
  (286 shorter events, 202.8 us)
Async XLA Ops:
  65.8 35.8 %collective-permute-start.17 = (bf16[4,256,512]{2,1,0:T(8,128)(2,1)}, bf16[4,256,512]{2,1,0:T(8,128)(2,1)}, u32[]{:S(2)}, u32[]{:S(2)}) collective-permute-start(bf16[4,256,512]{2,1,0:T(8,128)(2,1)} %bitcast.28.refs_0_), channel_id=1, source_target_pairs={{0,2},{1,3},{2,4},{3,5},{4,6},{5,7},{8,10},{9,11},{10,12},{11,13},... | collective-permute-start | bytes 3145736 | tf_op jit(solution)/shard_map/ppermute | solution.py:87
  103.6 33.9 %collective-permute-start.22 = (bf16[4,256,512]{2,1,0:T(8,128)(2,1)}, bf16[4,256,512]{2,1,0:T(8,128)(2,1)}, u32[]{:S(2)}, u32[]{:S(2)}) collective-permute-start(bf16[4,256,512]{2,1,0:T(8,128)(2,1)} %bitcast.28.refs_0_), channel_id=1, source_target_pairs={{0,1},{1,0},{2,3},{3,2},{4,5},{5,4},{6,7},{7,6},{8,9},{9,8},{10,11... | collective-permute-start | bytes 3145736 | tf_op jit(solution)/shard_map/ppermute | solution.py:87
  104.3 32.6 %collective-permute-start.21 = (bf16[1,2,64,4096]{3,2,1,0:T(8,128)(2,1)S(1)}, bf16[1,2,64,4096]{3,2,1,0:T(8,128)(2,1)S(1)}, u32[]{:S(2)}, u32[]{:S(2)}) collective-permute-start(bf16[1,2,64,4096]{3,2,1,0:T(8,128)(2,1)S(1)} %maximum_bitcast_fusion.1), channel_id=1, source_target_pairs={{0,16},{1,17},{2,18},{3,19},{4,20},{5,21},{6,22},{7,23},{8,24},{9,... | collective-permute-start | bytes 3145736 | tf_op jit(solution)/shard_map/ppermute | solution.py:87
  105.9 29.3 %collective-permute-start.20 = (bf16[1,2,64,4096]{3,2,1,0:T(8,128)(2,1)S(1)}, bf16[1,2,64,4096]{3,2,1,0:T(8,128)(2,1)S(1)}, u32[]{:S(2)}, u32[]{:S(2)}) collective-permute-start(bf16[1,2,64,4096]{3,2,1,0:T(8,128)(2,1)S(1)} %maximum_bitcast_fusion), channel_id=1, source_target_pairs={{0,8},{1,9},{2,10},{3,11},{4,12},{5,13},{6,14},{7,15},{8,0},{9,1},... | collective-permute-start | bytes 3145736 | tf_op jit(solution)/shard_map/ppermute | solution.py:87
  107.4 26.7 %collective-permute-start.24 = (bf16[4,256,512]{2,1,0:T(8,128)(2,1)}, bf16[4,256,512]{2,1,0:T(8,128)(2,1)}, u32[]{:S(2)}, u32[]{:S(2)}) collective-permute-start(bf16[4,256,512]{2,1,0:T(8,128)(2,1)} %collective-permute-done.17.refs_2_.refs_1_), channel_id=1, source_target_pairs={{0,2},{1,3},{2,4},{3,5},{4,6},{5,7},{8,10},{9,11},{10,12},{11,13},... | collective-permute-start | bytes 3145736 | tf_op jit(solution)/shard_map/ppermute | solution.py:87
  113.8 29.3 %collective-permute-start.23 = (bf16[4,256,512]{2,1,0:T(8,128)(2,1)}, bf16[4,256,512]{2,1,0:T(8,128)(2,1)}, u32[]{:S(2)}, u32[]{:S(2)}) collective-permute-start(bf16[4,256,512]{2,1,0:T(8,128)(2,1)} %collective-permute-done.17.refs_2_.refs_1_), channel_id=1, source_target_pairs={{0,1},{1,0},{2,3},{3,2},{4,5},{5,4},{6,7},{7,6},{8,9},{9,8},{10,11... | collective-permute-start | bytes 3145736 | tf_op jit(solution)/shard_map/ppermute | solution.py:87
  136.3 48.5 %collective-permute-start.26 = (bf16[2,2,64,4096]{3,2,1,0:T(8,128)(2,1)}, bf16[2,2,64,4096]{3,2,1,0:T(8,128)(2,1)}, u32[]{:S(2)}, u32[]{:S(2)}) collective-permute-start(bf16[2,2,64,4096]{3,2,1,0:T(8,128)(2,1)} %constant_dynamic-update-slice_fusion.rest_0_), channel_id=1, source_target_pairs={{0,16},{1,17},{2,18},{3,19},{4,20},{5,21},{6,22},{7,23},{8,24},{9,... | collective-permute-start | bytes 6291464 | tf_op jit(solution)/shard_map/ppermute | solution.py:87
  136.9 47.9 %collective-permute-start.27 = (bf16[2,2,64,4096]{3,2,1,0:T(8,128)(2,1)S(1)}, bf16[2,2,64,4096]{3,2,1,0:T(8,128)(2,1)}, u32[]{:S(2)}, u32[]{:S(2)}) collective-permute-start(bf16[2,2,64,4096]{3,2,1,0:T(8,128)(2,1)S(1)} %constant_dynamic-update-slice_fusion.2.rest_2_), channel_id=1, source_target_pairs={{0,8},{1,9},{2,10},{3,11},{4,12},{5,13},{6,14},{7,15},{8,0},{9,1},... | collective-permute-start | bytes 6291464 | tf_op jit(solution)/shard_map/ppermute | solution.py:87
  137.6 47.8 %collective-permute-start.30 = (bf16[4,256,512]{2,1,0:T(8,128)(2,1)}, bf16[4,256,512]{2,1,0:T(8,128)(2,1)}, u32[]{:S(2)}, u32[]{:S(2)}) collective-permute-start(bf16[4,256,512]{2,1,0:T(8,128)(2,1)} %collective-permute-done.24.refs_4_.refs_0_), channel_id=1, source_target_pairs={{0,2},{1,3},{2,4},{3,5},{4,6},{5,7},{8,10},{9,11},{10,12},{11,13},... | collective-permute-start | bytes 3145736 | tf_op jit(solution)/shard_map/ppermute | solution.py:87
  143.1 44.6 %collective-permute-start.28 = (bf16[2,2,64,4096]{3,2,1,0:T(8,128)(2,1)}, bf16[2,2,64,4096]{3,2,1,0:T(8,128)(2,1)}, u32[]{:S(2)}, u32[]{:S(2)}) collective-permute-start(bf16[2,2,64,4096]{3,2,1,0:T(8,128)(2,1)} %constant_dynamic-update-slice_fusion.rest_0_), channel_id=1, source_target_pairs={{0,1},{1,0},{2,3},{3,2},{4,5},{5,4},{6,7},{7,6},{8,9},{9,8},{10,11... | collective-permute-start | bytes 6291464 | tf_op jit(solution)/shard_map/ppermute | solution.py:87
  143.2 44.5 %collective-permute-start.29 = (bf16[2,2,64,4096]{3,2,1,0:T(8,128)(2,1)S(1)}, bf16[2,2,64,4096]{3,2,1,0:T(8,128)(2,1)}, u32[]{:S(2)}, u32[]{:S(2)}) collective-permute-start(bf16[2,2,64,4096]{3,2,1,0:T(8,128)(2,1)S(1)} %constant_dynamic-update-slice_fusion.2.rest_2_), channel_id=1, source_target_pairs={{0,1},{1,0},{2,3},{3,2},{4,5},{5,4},{6,7},{7,6},{8,9},{9,8},{10,11... | collective-permute-start | bytes 6291464 | tf_op jit(solution)/shard_map/ppermute | solution.py:87
  291.7 38.1 %collective-permute-start.37 = (bf16[4,256,512]{2,1,0:T(8,128)(2,1)}, bf16[4,256,512]{2,1,0:T(8,128)(2,1)}, u32[]{:S(2)}, u32[]{:S(2)}) collective-permute-start(bf16[4,256,512]{2,1,0:T(8,128)(2,1)} %fusion.5), channel_id=1, source_target_pairs={{2,0},{3,1},{4,2},{5,3},{6,4},{7,5},{10,8},{11,9},{12,10},{13,11},... | collective-permute-start | bytes 3145736 | tf_op jit(solution)/shard_map/ppermute | solution.py:87
  298.7 40.5 %collective-permute-start.39 = (bf16[2,2,64,3072]{3,2,1,0:T(8,128)(2,1)}, bf16[2,2,64,3072]{3,2,1,0:T(8,128)(2,1)}, u32[]{:S(2)}, u32[]{:S(2)}) collective-permute-start(bf16[2,2,64,3072]{3,2,1,0:T(8,128)(2,1)} %fusion.3), channel_id=1, source_target_pairs={{0,16},{1,17},{2,18},{3,19},{4,20},{5,21},{6,22},{7,23},{8,24},{9,... | collective-permute-start | bytes 4718600 | tf_op jit(solution)/shard_map/ppermute | solution.py:87
  302.0 44.6 %collective-permute-start.40 = (bf16[2,2,64,3072]{3,2,1,0:T(8,128)(2,1)}, bf16[2,2,64,3072]{3,2,1,0:T(8,128)(2,1)}, u32[]{:S(2)}, u32[]{:S(2)}) collective-permute-start(bf16[2,2,64,3072]{3,2,1,0:T(8,128)(2,1)} %add_convert_fusion), channel_id=1, source_target_pairs={{0,8},{1,9},{2,10},{3,11},{4,12},{5,13},{6,14},{7,15},{8,0},{9,1},... | collective-permute-start | bytes 4718600 | tf_op jit(solution)/shard_map/ppermute | solution.py:87
  333.4 41.4 %collective-permute-start.38 = (bf16[4,256,512]{2,1,0:T(8,128)(2,1)S(1)}, bf16[4,256,512]{2,1,0:T(8,128)(2,1)}, u32[]{:S(2)}, u32[]{:S(2)}) collective-permute-start(bf16[4,256,512]{2,1,0:T(8,128)(2,1)S(1)} %fusion), channel_id=1, source_target_pairs={{2,0},{3,1},{4,2},{5,3},{6,4},{7,5},{10,8},{11,9},{12,10},{13,11},... | collective-permute-start | bytes 3145736 | tf_op jit(solution)/shard_map/ppermute | solution.py:87
  334.7 42.1 %collective-permute-start.36 = (bf16[2,4,256,512]{3,2,1,0:T(8,128)(2,1)}, bf16[2,4,256,512]{3,2,1,0:T(8,128)(2,1)}, u32[]{:S(2)}, u32[]{:S(2)}) collective-permute-start(bf16[2,4,256,512]{3,2,1,0:T(8,128)(2,1)} %get-tuple-element.178), channel_id=1, source_target_pairs={{0,1},{1,0},{2,3},{3,2},{4,5},{5,4},{6,7},{7,6},{8,9},{9,8},{10,11... | collective-permute-start | bytes 6291464 | tf_op jit(solution)/shard_map/ppermute | solution.py:87
  342.1 40.6 %collective-permute-start.42 = (bf16[1,2,64,3072]{3,2,1,0:T(8,128)(2,1)}, bf16[1,2,64,3072]{3,2,1,0:T(8,128)(2,1)S(1)}, u32[]{:S(2)}, u32[]{:S(2)}) collective-permute-start(bf16[1,2,64,3072]{3,2,1,0:T(8,128)(2,1)} %fusion.4), channel_id=1, source_target_pairs={{0,8},{1,9},{2,10},{3,11},{4,12},{5,13},{6,14},{7,15},{8,0},{9,1},... | collective-permute-start | bytes 2359304 | tf_op jit(solution)/shard_map/ppermute | solution.py:87
  348.9 33.7 %collective-permute-start.43 = (bf16[1,2,64,3072]{3,2,1,0:T(8,128)(2,1)}, bf16[1,2,64,3072]{3,2,1,0:T(8,128)(2,1)}, u32[]{:S(2)}, u32[]{:S(2)}) collective-permute-start(bf16[1,2,64,3072]{3,2,1,0:T(8,128)(2,1)} %add_convert_fusion.5), channel_id=1, source_target_pairs={{0,16},{1,17},{2,18},{3,19},{4,20},{5,21},{6,22},{7,23},{8,24},{9,... | collective-permute-start | bytes 2359304 | tf_op jit(solution)/shard_map/ppermute | solution.py:87
  374.3 75.4 %collective-permute-start.45 = (bf16[2,4,2,64,2048]{4,3,2,1,0:T(8,128)(2,1)}, bf16[2,4,2,64,2048]{4,3,2,1,0:T(8,128)(2,1)}, u32[]{:S(2)}, u32[]{:S(2)}) collective-permute-start(bf16[2,4,2,64,2048]{4,3,2,1,0:T(8,128)(2,1)} %get-tuple-element.190), channel_id=1, source_target_pairs={{0,1},{1,0},{2,3},{3,2},{4,5},{5,4},{6,7},{7,6},{8,9},{9,8},{10,11... | collective-permute-start | bytes 12582920 | tf_op jit(solution)/shard_map/ppermute | solution.py:87
  381.4 65.6 %collective-permute-start.41 = (bf16[4,256,512]{2,1,0:T(8,128)(2,1)}, bf16[4,256,512]{2,1,0:T(8,128)(2,1)S(1)}, u32[]{:S(2)}, u32[]{:S(2)}) collective-permute-start(bf16[4,256,512]{2,1,0:T(8,128)(2,1)} %fusion.1), channel_id=1, source_target_pairs={{2,0},{3,1},{4,2},{5,3},{6,4},{7,5},{10,8},{11,9},{12,10},{13,11},... | collective-permute-start | bytes 3145736 | tf_op jit(solution)/shard_map/ppermute | solution.py:87
  386.7 59.3 %collective-permute-start.44 = (bf16[64,3072]{1,0:T(8,128)(2,1)S(1)}, bf16[64,3072]{1,0:T(8,128)(2,1)S(1)}, u32[]{:S(2)}, u32[]{:S(2)}) collective-permute-start(bf16[64,3072]{1,0:T(8,128)(2,1)S(1)} %fusion.38), channel_id=1, source_target_pairs={{0,2},{1,3},{2,4},{3,5},{4,6},{5,7},{6,0},{7,1},{8,10},{9,11},{10,... | collective-permute-start | bytes 1179656 | tf_op jit(solution)/shard_map/ppermute | solution.py:87
  472.8 28.2 %collective-permute-start.54 = (bf16[2,4,2,64,512]{4,3,2,1,0:T(8,128)(2,1)}, bf16[2,4,2,64,512]{4,3,2,1,0:T(8,128)(2,1)S(1)}, u32[]{:S(2)}, u32[]{:S(2)}) collective-permute-start(bf16[2,4,2,64,512]{4,3,2,1,0:T(8,128)(2,1)} %get-tuple-element.207), channel_id=1, source_target_pairs={{0,1},{1,0},{2,3},{3,2},{4,5},{5,4},{6,7},{7,6},{8,9},{9,8},{10,11... | collective-permute-start | bytes 3145736 | tf_op jit(solution)/shard_map/ppermute | solution.py:87
  472.9 27.6 %collective-permute-start.63 = (f32[2,128]{1,0:T(2,128)S(1)}, f32[2,128]{1,0:T(2,128)S(1)}, u32[]{:S(2)}, u32[]{:S(2)}) collective-permute-start(f32[2,128]{1,0:T(2,128)S(1)} %pad_maximum_fusion.11), channel_id=1, source_target_pairs={{0,8},{1,9},{2,10},{3,11},{4,12},{5,13},{6,14},{7,15},{8,0},{9,1},... | collective-permute-start | bytes 3080 | tf_op jit(solution)/shard_map/ppermute | solution.py:87
  485.7 32.2 %collective-permute-start.50 = (bf16[1,2,64,2048]{3,2,1,0:T(8,128)(2,1)}, bf16[1,2,64,2048]{3,2,1,0:T(8,128)(2,1)}, u32[]{:S(2)}, u32[]{:S(2)}) collective-permute-start(bf16[1,2,64,2048]{3,2,1,0:T(8,128)(2,1)} %add_convert_fusion.6), channel_id=1, source_target_pairs={{0,16},{1,17},{2,18},{3,19},{4,20},{5,21},{6,22},{7,23},{8,24},{9,... | collective-permute-start | bytes 1572872 | tf_op jit(solution)/shard_map/ppermute | solution.py:87
  (71 other events, 764.8 us)
